TPU v7x, 32 devices: a whole 2x2x4 slice. The times are simulated.
32 devices in a mesh: dp: 16 (over z, y, core), head: 2 (over x).
Axes of the slice: x: 2, y: 2, z: 4, core: 2. Of those that a mesh axis runs over, the one named last changes fastest.
Arguments:
- tokens: bfloat16 [32768, 768], P(('dp', 'head')), may hold values from -6 to 6
- labels: int32 [64, 512], P('dp'), may hold values from 0 to 3, never falling along the last dimension, each value on 1 to 256 neighbouring positions
- micro_counts: int32 [16], P('dp'), may hold values from 1 to 4, as said below
- w_query: bfloat16 [768, 768], P(None, 'head'), may hold values from -0.4375 to 0.4375
- b_query: bfloat16 [768], P('head'), may hold values from -3 to 3
- w_key: bfloat16 [768, 768], P(None, 'head'), may hold values from -0.21875 to 0.21875
- w_value: bfloat16 [768, 768], P(None, 'head'), may hold values from -0.21875 to 0.21875
- b_value: bfloat16 [768], P('head'), may hold values from -3 to 3
- w_out: bfloat16 [768, 768], replicated, may hold values from -0.625 to 0.625
- b_out: float32 [768], replicated, may hold values from -2 to 2
- gain_one: float32 [768], replicated, may hold values from 0.5 to 1.5
- shift_one: float32 [768], replicated, may hold values from -2 to 2
- w_up: bfloat16 [768, 3072], replicated, may hold values from -0.21875 to 0.21875
- b_up: float32 [3072], replicated, may hold values from -2 to 2
- w_down: bfloat16 [3072, 768], replicated, may hold values from -0.109375 to 0.109375
- b_down: float32 [768], replicated, may hold values from -2 to 2
- gain_two: float32 [768], replicated, may hold values from 0.5 to 1.5
- shift_two: float32 [768], replicated, may hold values from -2 to 2
- cotangent: bfloat16 [32768, 768], P(('dp', 'head')), may hold values from -6 to 6
Outputs:
- layer_output: bfloat16 [32768, 768], P(('dp', 'head'))
- grad_tokens: float32 [32768, 768], P(('dp', 'head'))
- grad_w_query: float32 [768, 768], P(None, 'head')
- grad_b_query: float32 [768], P('head')
- grad_w_key: float32 [768, 768], P(None, 'head')
- grad_w_value: float32 [768, 768], P(None, 'head')
- grad_b_value: float32 [768], P('head')
- grad_w_out: float32 [768, 768], replicated
- grad_b_out: float32 [768], replicated
- grad_gain_one: float32 [768], replicated
- grad_shift_one: float32 [768], replicated
- grad_w_up: float32 [768, 3072], P(None, ('dp', 'head'))
- grad_b_up: float32 [3072], replicated
- grad_w_down: float32 [3072, 768], P(('dp', 'head'))
- grad_b_down: float32 [768], replicated
- grad_gain_two: float32 [768], replicated
- grad_shift_two: float32 [768], replicated
Inputs may be any that keep to these rules, and one draw needn't show every extreme that they name: `micro_counts`: each entry counts the leading micro-batches of its data group, of 4; some group has 4 and some has 1. `labels`: document numbers never fall along a sequence; a document has at most 256 positions.
All inputs are finite; a program needn't handle non-finite values.
Results may differ from a plain program's by a relative error of at most 0.014.
The roundings to bfloat16 on the way count: a program that leaves them out, or rounds other values in their place, can miss the bound.
Values may be sent and summed in bfloat16 or wider, within the bound.
No kernel may reach another device: no remote copies, remote signals or barrier semaphores. Data moves between devices by JAX's collectives and lax.ppermute only.
A program may use at most 192 MiB of HBM per device.

v0:
```python
import jax
import jax.numpy as jnp
from jax import lax
from jax.sharding import PartitionSpec as P

HEAD_DIM = 64
MICRO = 4


norm_eps = 1e-05


def contract_rows(left, right):
    return lax.dot_general(
        left, right, (((0,), (0,)), ((), ())), preferred_element_type=jnp.float32
    )


def contract_cols(left, right):
    return lax.dot_general(
        left, right, (((1,), (1,)), ((), ())), preferred_element_type=jnp.float32
    )


def project(source, weight, offset):
    result = jnp.dot(source, weight, preferred_element_type=jnp.float32)
    if offset is not None:
        result = result + offset.astype(jnp.float32)
    return result.astype(jnp.bfloat16)


def norm_parts(values, gain, shift):
    average = jnp.mean(values, axis=-1, keepdims=True)
    centered = values - average
    factor = lax.rsqrt(jnp.mean(centered * centered, axis=-1, keepdims=True) + norm_eps)
    normed = centered * factor
    return (normed * gain + shift, normed, factor)


def norm_back(grad_out, normed, factor, gain):
    scaled = grad_out * gain
    grad_in = factor * (
        scaled
        - jnp.mean(scaled, axis=-1, keepdims=True)
        - normed * jnp.mean(scaled * normed, axis=-1, keepdims=True)
    )
    return (grad_in, jnp.sum(grad_out * normed, 0), jnp.sum(grad_out, 0))


def masked_scores(query_rows, key_rows, marks):
    scores = (
        jnp.einsum("qhd,khd->hqk", query_rows, key_rows, preferred_element_type=jnp.float32) * 0.125
    )
    allowed = marks[:, None] == marks[None, :]
    return jnp.where(allowed[None], scores, -1000000000.0)


def attend_forward(inputs):
    query_rows, key_rows, value_rows, marks = inputs
    scores = masked_scores(query_rows, key_rows, marks)
    largest = jnp.max(scores, axis=-1, keepdims=True)
    exponent = jnp.exp(scores - largest)
    row_total = jnp.sum(exponent, axis=-1, keepdims=True)
    softened = (exponent / row_total).astype(jnp.bfloat16)
    context = jnp.einsum("hqk,khd->qhd", softened, value_rows, preferred_element_type=jnp.float32)
    return (context.astype(jnp.bfloat16), (largest + jnp.log(row_total))[..., 0])


def attend_backward(inputs):
    query_rows, key_rows, value_rows, marks, logsum, grad_context = inputs
    scores = masked_scores(query_rows, key_rows, marks)
    softened = jnp.exp(scores - logsum[..., None])
    grad_soft = jnp.einsum(
        "qhd,khd->hqk", grad_context, value_rows, preferred_element_type=jnp.float32
    )
    grad_values = jnp.einsum(
        "hqk,qhd->khd",
        softened.astype(jnp.bfloat16),
        grad_context,
        preferred_element_type=jnp.float32,
    )
    row_inner = jnp.sum(softened * grad_soft, axis=-1, keepdims=True)
    grad_scores = (softened * (grad_soft - row_inner)).astype(jnp.bfloat16)
    grad_queries = (
        jnp.einsum("hqk,khd->qhd", grad_scores, key_rows, preferred_element_type=jnp.float32)
        * 0.125
    )
    grad_keys = (
        jnp.einsum("hqk,qhd->khd", grad_scores, query_rows, preferred_element_type=jnp.float32)
        * 0.125
    )
    return (
        grad_queries.astype(jnp.bfloat16),
        grad_keys.astype(jnp.bfloat16),
        grad_values.astype(jnp.bfloat16),
    )


def exact_gelu(values):
    return jax.nn.gelu(values, approximate=False)


def shards(
    tokens,
    labels,
    micro_counts,
    w_query,
    b_query,
    w_key,
    w_value,
    b_value,
    w_out,
    b_out,
    gain_one,
    shift_one,
    w_up,
    b_up,
    w_down,
    b_down,
    gain_two,
    shift_two,
    cotangent,
):
    local_rows = tokens.shape[0]
    seq_len = labels.shape[1]
    full_query, full_key, full_value, full_bquery, full_bvalue = (
        w_query,
        w_key,
        w_value,
        b_query,
        b_value,
    )
    attend_in = lax.all_gather(tokens, "head", axis=0, tiled=True)
    in_rows = attend_in.shape[0]
    head_count = full_query.shape[1] // HEAD_DIM
    width = head_count * HEAD_DIM
    shape_four = (labels.shape[0], seq_len, head_count, HEAD_DIM)
    query_rows = project(attend_in, full_query, full_bquery).reshape(shape_four)
    key_rows = project(attend_in, full_key, None).reshape(shape_four)
    value_rows = project(attend_in, full_value, full_bvalue).reshape(shape_four)
    context, logsum = lax.map(attend_forward, (query_rows, key_rows, value_rows, labels))
    context = context.reshape(in_rows, width)
    mixed_ctx = lax.all_to_all(context, "head", split_axis=0, concat_axis=1, tiled=True)
    attended = jnp.dot(mixed_ctx, w_out, preferred_element_type=jnp.float32) + b_out
    hidden, normed_one, factor_one = norm_parts(
        tokens.astype(jnp.float32) + attended, gain_one, shift_one
    )
    hidden_low = hidden.astype(jnp.bfloat16)
    inner = jnp.dot(hidden_low, w_up, preferred_element_type=jnp.float32) + b_up
    activated, gelu_back = jax.vjp(exact_gelu, inner)
    activated_low = activated.astype(jnp.bfloat16)
    branch = jnp.dot(activated_low, w_down, preferred_element_type=jnp.float32) + b_down
    result, normed_two, factor_two = norm_parts(hidden + branch, gain_two, shift_two)
    layer_output = result.astype(jnp.bfloat16)
    position = jnp.arange(local_rows, dtype=jnp.int32) % seq_len
    live = (position // (seq_len // MICRO) < micro_counts[0]).astype(jnp.float32)
    grad_y = cotangent.astype(jnp.float32) * live[:, None]
    grad_mid, grad_gain_two, grad_shift_two = norm_back(grad_y, normed_two, factor_two, gain_two)
    grad_b_down = jnp.sum(grad_mid, 0)
    grad_mid_low = grad_mid.astype(jnp.bfloat16)
    down_turned = contract_rows(grad_mid_low, activated_low)
    grad_activ = contract_cols(grad_mid_low, w_down)
    grad_inner = gelu_back(grad_activ)[0].astype(jnp.bfloat16)
    grad_b_up = jnp.sum(grad_inner.astype(jnp.float32), 0)
    up_local = contract_rows(hidden_low, grad_inner)
    grad_hidden = grad_mid + contract_cols(grad_inner, w_up)
    grad_first, grad_gain_one, grad_shift_one = norm_back(
        grad_hidden, normed_one, factor_one, gain_one
    )
    grad_b_out = jnp.sum(grad_first, 0)
    grad_first_low = grad_first.astype(jnp.bfloat16)
    out_local = contract_rows(mixed_ctx, grad_first_low)
    grad_context = contract_cols(grad_first_low, w_out).astype(jnp.bfloat16)
    grad_heads = lax.all_to_all(grad_context, "head", split_axis=1, concat_axis=0, tiled=True)
    grad_queries, grad_keys, grad_values = lax.map(
        attend_backward,
        (query_rows, key_rows, value_rows, labels, logsum, grad_heads.reshape(shape_four)),
    )
    grad_queries = grad_queries.reshape(in_rows, width)
    grad_keys = grad_keys.reshape(in_rows, width)
    grad_values = grad_values.reshape(in_rows, width)
    query_local = contract_rows(attend_in, grad_queries)
    key_local = contract_rows(attend_in, grad_keys)
    value_local = contract_rows(attend_in, grad_values)
    bquery_local = jnp.sum(grad_queries.astype(jnp.float32), 0)
    bvalue_local = jnp.sum(grad_values.astype(jnp.float32), 0)
    grad_rows = (
        contract_cols(grad_queries, full_query)
        + contract_cols(grad_keys, full_key)
        + contract_cols(grad_values, full_value)
    )
    grad_tokens = grad_first + lax.psum_scatter(grad_rows, "head", scatter_dimension=0, tiled=True)
    grad_w_query, grad_b_query, grad_w_key, grad_w_value, grad_b_value = lax.psum(
        (query_local, bquery_local, key_local, value_local, bvalue_local), "dp"
    )
    (
        grad_w_out,
        grad_b_out,
        grad_gain_one,
        grad_shift_one,
        grad_b_up,
        grad_b_down,
        grad_gain_two,
        grad_shift_two,
    ) = lax.psum(
        (
            out_local,
            grad_b_out,
            grad_gain_one,
            grad_shift_one,
            grad_b_up,
            grad_b_down,
            grad_gain_two,
            grad_shift_two,
        ),
        ("dp", "head"),
    )
    grad_w_up, down_slice = (
        lax.psum_scatter(up_local, ("dp", "head"), scatter_dimension=1, tiled=True),
        lax.psum_scatter(down_turned, ("dp", "head"), scatter_dimension=1, tiled=True),
    )
    grad_w_down = jnp.transpose(down_slice)
    return (
        layer_output,
        grad_tokens,
        grad_w_query,
        grad_b_query,
        grad_w_key,
        grad_w_value,
        grad_b_value,
        grad_w_out,
        grad_b_out,
        grad_gain_one,
        grad_shift_one,
        grad_w_up,
        grad_b_up,
        grad_w_down,
        grad_b_down,
        grad_gain_two,
        grad_shift_two,
    )


def solution(mesh):
    placed = (
        P(("dp", "head"), None),
        P("dp", None),
        P("dp"),
        P(None, "head"),
        P("head"),
        P(None, "head"),
        P(None, "head"),
        P("head"),
        P(),
        P(),
        P(),
        P(),
        P(),
        P(),
        P(),
        P(),
        P(),
        P(),
        P(("dp", "head"), None),
    )
    return jax.shard_map(
        shards,
        mesh=mesh,
        in_specs=placed,
        out_specs=(
            P(("dp", "head"), None),
            P(("dp", "head"), None),
            P(None, "head"),
            P("head"),
            P(None, "head"),
            P(None, "head"),
            P("head"),
            P(),
            P(),
            P(),
            P(),
            P(None, ("dp", "head")),
            P(),
            P(("dp", "head"), None),
            P(),
            P(),
            P(),
        ),
        check_vma=False,
    )
```

profile of v0, /device:TPU:0, one launch (start us, length us, event | category | flops | bytes accessed | tf_op | source)
XLA Modules:
  0.0 999.7 jit_solution(16152266388126480959)
XLA Ops:
  9.3 47.9 %all-gather.2.cloned.1.call-done = bf16[2048,768]{1,0:T(8,128)(2,1)} async-done(((bf16[1024,768]{1,0:T(8,128)(2,1)}), bf16[2048,768]{1,0:T(8,128)(2,1)}) %all-gather.2.cloned.1.call-update) | async-done | bytes 3145744 | tf_op jit(solution)/shard_map/all_gather | solution.py:133
  57.2 5.0 add_convert_fusion.3
  68.7 3.0 add_convert_fusion.2
  74.2 3.9 reshape.230
  78.1 3.0 copy.99
  81.2 3.0 convolution_convert_fusion
  86.7 3.8 reshape.231
  90.6 2.9 copy.100
  94.8 31.8 %while.26 = (s32[]{:T(128)}, bf16[4,512,6,64]{1,3,2,0:T(8,128)(2,1)}, f32[4,6,512]{2,1,0:T(8,128)}, bf16[4,512,6,64]{1,3,2,0:T(8,128)(2,1)S(1)}, s32[4,512]{1,0:...) while((s32[]{:T(128)}, bf16[4,512,6,64]{1,3,2,0:T(8,128)(2,1)}, ...), condition=%wide.region_3.4_spmd, body=%wide.region_0.3_spmd.sunk | while | flops 421983232 | bytes 21614692 | solution.py:141
  126.6 4.3 copy.101
  130.9 4.9 all_to_all.26
  135.8 3.0 copy.102
  138.8 4.8 all-to-all-start
  147.7 15.4 %all-to-all-done = bf16[2,1024,384]{1,2,0:T(8,128)(2,1)} async-done(((bf16[2,1024,384]{1,2,0:T(8,128)(2,1)}), bf16[2,1024,384]{1,2,0:T(8,128)(2,1)}, u32[]{:S(2)}, u32[]{:S(2)}) %all-to-all-start) | async-done | bytes 1572896 | tf_op jit(solution)/shard_map/all_to_all | solution.py:143
  163.1 3.7 fusion.90
  167.7 35.8 %multiply_convert_fusion.1 = (bf16[1024,3072]{1,0:T(8,128)(2,1)}, f32[1024,3072]{1,0:T(8,128)}, f32[1024,3072]{1,0:T(8,128)}) fusion(f32[3072]{0:T(1024)S(1)} %copy-done.34, bf16[768,3072]{1,0:T(8,128)(2,1)S(1)} %bitcast.192, f32[1024,768]{0,1:T(8,128)S(1)} %get-tuple-element.281, f32[768]{0:T(1024)S(1)} %copy-done.37, f32[768]{0:T(1024)S(1)} %copy-done.27, ...), kind=kOutput, calls=%fused_computation.70 | convolution fusion | flops 5043388416 | bytes 39348224 | tf_op jit(solution)/shard_map/dot_general | solution.py:149
  203.5 17.9 %fusion.91 = (f32[1024]{0:T(1024)S(1)}, f32[1024,768]{0,1:T(8,128)S(1)}) fusion(f32[768]{0:T(1024)S(1)} %copy-done.36, bf16[1024,3072]{1,0:T(8,128)(2,1)} %get-tuple-element.273, bf16[3072,768]{1,0:T(8,128)(2,1)S(1)} %bitcast.190, f32[768]{0:T(1024)S(1)} %copy-done.37, f32[768]{0:T(1024)S(1)} %copy-done.27, f32[1024]{0:T(1024)S(1)} %add_rsqrt_fusion.1, ...), kind=kOutput, calls=%fused_computation.149 | convolution fusion | flops 4837342208 | bytes 17323008 | tf_op jit(solution)/shard_map/dot_general | solution.py:152
  223.1 21.2 %convert_reduce_fusion = (f32[3072]{0:T(1024)}, bf16[1024,3072]{1,0:T(8,128)(2,1)}) fusion(f32[1024,3072]{1,0:T(8,128)} %get-tuple-element.274, bf16[3072,768]{1,0:T(8,128)(2,1)} %param.37, f32[1024]{0:T(1024)S(1)} %get-tuple-element.288, f32[1024,768]{0,1:T(8,128)} %copy-done.1, f32[1024]{0:T(1024)S(1)} %broadcast_multiply_fusion.4, ...), kind=kOutput, calls=%fused_computation.68 | convolution fusion | flops 4893176832 | bytes 40942592 | tf_op jit(solution)/shard_map/dot_general | solution.py:20
  244.3 12.5 %multiply_reduce_fusion.2 = (f32[768]{0:T(1024)}, f32[1024]{0:T(1024)S(1)}, f32[1024]{0:T(1024)S(1)}, f32[768]{0:T(1024)}, f32[1024,768]{0,1:T(8,128)S(1)}) fusion(f32[1024,768]{0,1:T(8,128)} %copy-done.6, f32[1024]{0:T(1024)S(1)} %add_rsqrt_fusion.1, f32[1024]{0:T(1024)S(1)} %broadcast_multiply_fusion.5, f32[768]{0:T(1024)S(1)} %copy-done.27, ...), kind=kOutput, calls=%fused_computation.86 | convolution fusion | flops 4846776320 | bytes 22069248 | tf_op jit(solution)/shard_map/dot_general | solution.py:20
  259.6 21.3 %all_to_all.35 = bf16[1024,2,384]{0,2,1:T(8,128)(2,1)S(1)} all-to-all(bf16[1024,2,384]{0,2,1:T(8,128)(2,1)S(1)} %bitcast.186), channel_id=1, replica_groups=mesh['dp'=16,'head'=2] {'head'}, dimensions={1} | all-to-all | bytes 3145728 | tf_op jit(solution)/shard_map/all_to_all | solution.py:174
  290.2 74.2 %while.27 = (s32[]{:T(128)}, bf16[4,512,6,64]{1,3,2,0:T(8,128)(2,1)}, bf16[4,512,6,64]{1,3,2,0:T(8,128)(2,1)}, bf16[4,512,6,64]{1,3,2,0:T(8,128)(2,1)}, bf16[4,5...) while((s32[]{:T(128)}, ...), condition=%wide.region_14.15_spmd, body=%wide.region_12.14_spmd.sunk | while | flops 1031468032 | bytes 64851124 | solution.py:175
  294.6 3.2 multiply_reduce_fusion.9
  302.2 2.8 fusion.156
  305.0 3.7 fusion.157
  313.1 3.2 multiply_reduce_fusion.9
  320.6 2.8 fusion.156
  323.5 3.7 fusion.157
  331.5 3.2 multiply_reduce_fusion.9
  339.1 2.8 fusion.156
  341.9 3.7 fusion.157
  350.0 3.2 multiply_reduce_fusion.9
  357.6 2.8 fusion.156
  360.4 3.7 fusion.157
  383.8 4.5 add_add_fusion
  388.4 5.3 fusion.69
  393.7 11.1 %fusion.83 = f32[768,3072]{0,1:T(8,128)} fusion(bf16[1024,3072]{1,0:T(8,128)(2,1)} %get-tuple-element.287, f32[1024,768]{0,1:T(8,128)} %copy-done.6, f32[768]{0:T(1024)S(1)} %copy-done.38, f32[768]{0:T(1024)S(1)} %copy-done.27, f32[1024]{0:T(1024)S(1)} %add_rsqrt_fusion.1, f32[1024]{0:T(1024)S(1)} %broadcast_multiply_fusion.5), kind=kOutput, calls=%fused_computation.144 | convolution fusion | flops 4835770368 | bytes 18888704 | tf_op jit(solution)/shard_map/dot_general | solution.py:14
  406.3 11.3 %fusion.72 = f32[768,3072]{0,1:T(8,128)} fusion(bf16[1024,3072]{1,0:T(8,128)(2,1)} %get-tuple-element.273, bf16[1024,768]{0,1:T(8,128)(2,1)S(1)} %copy-done.5, f32[1024,768]{0,1:T(8,128)} %copy-done.1, f32[1024]{0:T(1024)S(1)} %get-tuple-element.288, f32[1024]{0:T(1024)S(1)} %get-tuple-element.289, f32[1024]{0:T(1024)S(1)} %fusion.80, ...), kind=kOutput, calls=%fused_computation.118 | convolution fusion | flops 4839702528 | bytes 20470784 | tf_op jit(solution)/shard_map/dot_general | solution.py:14
  418.2 4.5 multiply_reduce_fusion.1
  425.4 40.9 %all-reduce = (f32[768]{0:T(1024)}, f32[768]{0:T(1024)}, f32[768]{0:T(1024)}, f32[3072]{0:T(1024)}, f32[768]{0:T(1024)}, /*index=5*/f32[768]{0:T(1024)}, f32[768]{0:T(1024)}) all-reduce(f32[768]{0:T(1024)S(1)} %get-tuple-element.271, f32[768]{0:T(1024)S(1)} %copy-done.29, ...), channel_id=1, replica_groups=mesh['dp'=16,'head'=2] {'dp','head'}, use_global_device_ids=true, to_apply=%region_25.26 | all-reduce | flops 7680 | bytes 61440 | tf_op jit(solution)/shard_map/psum | solution.py:205
  468.5 33.1 %all-reduce.1 = (f32[384]{0:T(512)}, f32[384]{0:T(512)}) all-reduce(f32[384]{0:T(512)S(1)} %reduce_sum.184, f32[384]{0:T(512)S(1)} %reduce_sum.186), channel_id=1, replica_groups=mesh['dp'=16,'head'=2] {'dp'}, use_global_device_ids=true, to_apply=%region_18.19 | all-reduce | flops 768 | bytes 6144 | tf_op jit(solution)/shard_map/psum | solution.py:193
  501.6 2.8 copy.119
  507.2 57.3 %reduce-scatter.4.cloned.1.call-done = f32[1024,768]{0,1:T(8,128)} async-done(((f32[2048,768]{0,1:T(8,128)}), f32[1024,768]{0,1:T(8,128)}) %reduce-scatter.4.cloned.1.call-update) | async-done | bytes 3145744 | tf_op jit(solution)/shard_map/reduce_scatter | solution.py:192
  564.5 5.5 add.180
  570.0 3.5 copy.118
  573.6 133.0 %all-reduce.6.cloned.1.call-done = f32[768,768]{1,0:T(8,128)} async-done(((f32[768,768]{1,0:T(8,128)}), f32[768,768]{1,0:T(8,128)}) %all-reduce.6.cloned.1.call-update) | async-done | bytes 2359312 | tf_op jit(solution)/shard_map/psum | solution.py:205
  706.5 140.8 %reduce-scatter.6.cloned.1.call-done = f32[768,96]{0,1:T(8,128)} async-done(((f32[768,3072]{0,1:T(8,128)}), f32[768,96]{0,1:T(8,128)}) %reduce-scatter.6.cloned.1.call-update) | async-done | bytes 294928 | tf_op jit(solution)/shard_map/reduce_scatter | solution.py:219
  847.3 142.1 %reduce-scatter.8.cloned.1.call-done = f32[768,96]{0,1:T(8,128)} async-done(((f32[768,3072]{0,1:T(8,128)}), f32[768,96]{0,1:T(8,128)}) %reduce-scatter.8.cloned.1.call-update) | async-done | bytes 294928 | tf_op jit(solution)/shard_map/reduce_scatter | solution.py:220
  989.4 3.2 copy.167
  (209 shorter events, 128.2 us)
Async XLA Ops:
  7.2 155.9 %copy-start = (bf16[768,768]{1,0:T(8,128)(2,1)S(1)}, bf16[768,768]{1,0:T(8,128)(2,1)}, u32[]{:S(2)}) copy-start(bf16[768,768]{1,0:T(8,128)(2,1)} %param.31) | copy-start | bytes 3538948
  7.2 50.0 %all-gather.2.cloned.1.call-start = ((), (), s32[]{:S(2)}) async-start(), calls=%async_computation.5 | async-start | bytes 4718592 | tf_op jit(solution)/shard_map/all_gather | solution.py:133
  63.9 4.3 copy-start.20
  66.3 2.4 copy-start.31
  74.2 7.0 copy-start.22
  78.1 3.1 copy-start.32
  126.5 9.2 copy-start.9
  138.8 4.9 copy-start.12
  138.8 24.4 %all-to-all-start = ((bf16[2,1024,384]{1,2,0:T(8,128)(2,1)}), bf16[2,1024,384]{1,2,0:T(8,128)(2,1)}, u32[]{:S(2)}, u32[]{:S(2)}) async-start(bf16[2,1024,384]{1,2,0:T(8,128)(2,1)} %copy.102), calls=%async_computation | async-start | bytes 3145728 | tf_op jit(solution)/shard_map/all_to_all | solution.py:143
  143.5 19.6 %copy-start.35 = (f32[768]{0:T(1024)S(1)}, f32[768]{0:T(1024)}, u32[]{:S(2)}) copy-start(f32[768]{0:T(1024)} %param.32) | copy-start | bytes 9220
  143.6 358.0 %all-reduce.8.cloned.1.call-start = ((), (), s32[]{:S(2)}) async-start(), calls=%async_computation.10 | async-start | bytes 7077888 | tf_op jit(solution)/shard_map/psum | solution.py:193
  147.0 97.3 %copy-start.4 = (bf16[1024,768]{0,1:T(8,128)(2,1)}, bf16[1024,768]{0,1:T(8,128)(2,1)S(1)}, u32[]{:S(2)}) copy-start(bf16[1024,768]{0,1:T(8,128)(2,1)S(1)} %copy.104) | copy-start | bytes 4718596
  163.1 4.2 slice-start.2
  163.1 4.2 slice-start.3
  163.1 40.4 %slice-start = ((s8[4718592]{0:T(1024)(128)(4,1)}), s8[4194304]{0:T(1024)(128)(4,1)S(1)}, s32[]{:S(2)}) async-start(s8[4718592]{0:T(1024)(128)(4,1)} %bitcast.189), calls=%async_computation.11 | async-start | bytes 8388608
  166.8 36.6 %copy-start.6 = (f32[1024,768]{0,1:T(8,128)}, f32[1024,768]{0,1:T(8,128)S(1)}, u32[]{:S(2)}) copy-start(f32[1024,768]{0,1:T(8,128)S(1)} %get-tuple-element.281) | copy-start | bytes 9437188
  167.7 35.8 %slice-start.1 = ((s8[4718592]{0:T(1024)(128)(4,1)}), s8[524288]{0:T(1024)(128)(4,1)S(1)}, s32[]{:S(2)}) async-start(s8[4718592]{0:T(1024)(128)(4,1)} %bitcast.189), calls=%async_computation.12 | async-start | bytes 1048576
  167.7 35.8 %copy-start.36 = (f32[768]{0:T(1024)S(1)}, f32[768]{0:T(1024)}, u32[]{:S(2)}) copy-start(f32[768]{0:T(1024)} %param.38) | copy-start | bytes 9220
  221.4 1.7 copy-start.1
  244.3 12.5 %copy-start.7 = (f32[1024,768]{0,1:T(8,128)S(1)}, f32[1024,768]{0,1:T(8,128)}, u32[]{:S(2)}) copy-start(f32[1024,768]{0,1:T(8,128)} %copy-done.6) | copy-start | bytes 9437188
  290.2 4.3 copy-start.10
  305.0 3.7 copy-start.11
  308.7 4.3 copy-start.10
  323.5 3.7 copy-start.11
  327.2 4.3 copy-start.10
  341.9 3.7 copy-start.11
  345.6 4.3 copy-start.10
  360.4 3.7 copy-start.11
  364.4 3.2 copy-start.17
  367.6 1.7 copy-start.3
  369.3 4.9 copy-start.13
  369.3 2.5 copy-start.33
  371.0 5.6 copy-start.15
  379.1 185.4 %reduce-scatter.4.cloned.1.call-start = ((), (), s32[]{:S(2)}) async-start(), calls=%async_computation.6 | async-start | bytes 9437184 | tf_op jit(solution)/shard_map/reduce_scatter | solution.py:192
  380.1 1.8 copy-start.14
  380.1 1.8 copy-start.23
  382.0 1.8 copy-start.16
  382.0 1.8 copy-start.24
  388.3 5.4 copy-start.38
  388.3 318.2 %all-reduce.6.cloned.1.call-start = ((), (), s32[]{:S(2)}) async-start(), calls=%async_computation.7 | async-start | bytes 4718592 | tf_op jit(solution)/shard_map/psum | solution.py:205
  393.7 453.6 %reduce-scatter.6.cloned.1.call-start = ((), (), s32[]{:S(2)}) async-start(), calls=%async_computation.8 | async-start | bytes 9732096 | tf_op jit(solution)/shard_map/reduce_scatter | solution.py:219
  404.9 584.5 %reduce-scatter.8.cloned.1.call-start = ((), (), s32[]{:S(2)}) async-start(), calls=%async_computation.9 | async-start | bytes 9732096 | tf_op jit(solution)/shard_map/reduce_scatter | solution.py:220
  422.7 2.7 copy-start.26
  422.7 2.7 copy-start.29
  422.7 2.7 copy-start.30
  422.7 43.6 %copy-start.2 = (bf16[4,512,6,64]{1,3,2,0:T(8,128)(2,1)S(1)}, bf16[4,512,6,64]{1,3,2,0:T(8,128)(2,1)}, u32[]{:S(2)}) copy-start(bf16[4,512,6,64]{1,3,2,0:T(8,128)(2,1)} %get-tuple-element.111) | copy-start | bytes 4718596
  501.6 2.8 copy-start.19
  501.6 4.2 copy-start.18
  (8 other events, 7.8 us)
Sparse Core Ops, SparseCore 0:
  9.6 47.6 all-gather.1
  379.2 106.8 all-reduce.7
  488.5 76.0 reduce-scatter.3
  571.4 135.0 all-reduce.5
  712.9 134.3 reduce-scatter.5
  854.6 134.7 reduce-scatter.7
where the time goes:
time: 1010 us; the launch traced here: 1000 us
  waiting for transfers between devices  537 us (53%)
  matrix products  226 us (22%)
  blocking collectives  95.3 us (9%)
  local copies, waits for them, and re-layouts  86.2 us (9%)
  other arithmetic  33.3 us (3%)
  between operations  15.5 us (2%)
    reduce_scatter x1, waiting for transfers between devices, shards(): lax.psum_scatter(down_turned, ('dp', 'head'), scatter_dimension=1, tiled=...  142 us
    reduce_scatter x1, waiting for transfers between devices, shards(): lax.psum_scatter(up_local, ('dp', 'head'), scatter_dimension=1, tiled=True)  141 us
    psum x1, waiting for transfers between devices, shards(): lax.psum((out_local, grad_b_out, grad_gain_one, grad_shift_one, grad_b_up...  133 us
    reduce_scatter x1, waiting for transfers between devices, shards(): lax.psum_scatter(grad_rows, 'head', scatter_dimension=0, tiled=True)  57.3 us
    all_gather x1, waiting for transfers between devices, shards(): attend_in = lax.all_gather(tokens, 'head', axis=0, tiled=True)  47.9 us
    dot_general x6, matrix products, contract_cols(): lax.dot_general(left, right, (((1,), (1,)), ((), ())), preferred_element_...  43.2 us
    psum x1, blocking collectives, shards(): lax.psum((out_local, grad_b_out, grad_gain_one, grad_shift_one, grad_b_up...  40.9 us
    dot_general x1, matrix products, shards(): inner = jnp.dot(hidden_low, w_up, preferred_element_type=jnp.float32) + b_up  35.8 us
  transfers between devices with their start and end apart: 7, of which 6 were waited for; matrix products, arithmetic and copies ran while one was open for 6% of the time, Pallas kernels for 0%

commit v1 on v0

v1 whole, which is shorter than its diff:
```python
import functools

import jax
import jax.numpy as jnp
from jax import lax
from jax.experimental import pallas as pl
from jax.experimental.pallas import tpu as pltpu
from jax.sharding import PartitionSpec as P

HEAD_DIM = 64
MICRO = 4
F32 = jnp.float32
BF16 = jnp.bfloat16
NORM_EPS = 1e-05
MASK = 2.0**30
AXES = ("dp", "head")


def dims(left, right, left_dim, right_dim):
    return lax.dot_general(
        left, right, (((left_dim,), (right_dim,)), ((), ())), preferred_element_type=F32
    )


def matmul(left, right):
    return jnp.dot(left, right, preferred_element_type=F32)


def query_marks(labels, shape):
    lane = lax.broadcasted_iota(jnp.int32, shape, 1)
    return jnp.where((lane & 63) == labels, 1.0, 0.0).astype(BF16)


def key_marks(labels, shape):
    lane = lax.broadcasted_iota(jnp.int32, shape, 1) & 63
    return jnp.where((lane < 4) & (lane != labels), -MASK, 0.0).astype(BF16)


def attend_forward(q_ref, k_ref, v_ref, lab_ref, out_ref, log_ref):
    labels = lab_ref[0]
    shape = (labels.shape[0], 128)
    low = lax.broadcasted_iota(jnp.int32, shape, 1) < HEAD_DIM
    q_extra, k_extra = query_marks(labels, shape), key_marks(labels, shape)
    q = q_ref[...] * jnp.asarray(0.125, BF16)
    k, v = k_ref[...], v_ref[...]
    outs = []
    for t in range(2):
        mine = low if t == 0 else jnp.logical_not(low)
        scores = dims(jnp.where(mine, k, k_extra), jnp.where(mine, q, q_extra), 1, 1)
        largest = jnp.max(scores, axis=0, keepdims=True)
        soft = jnp.exp(scores - largest)
        total = jnp.sum(soft, axis=0, keepdims=True)
        out = dims(v, soft.astype(BF16), 0, 0)
        outs.append(out[t * HEAD_DIM : (t + 1) * HEAD_DIM] * (1.0 / total))
        log_ref[0, 0, t : t + 1] = largest + jnp.log(total)
    out_ref[...] = jnp.concatenate(outs, axis=0).T.astype(BF16)


def run_attend_forward(qkv, labels, seq):
    rows = qkv.shape[0]
    pairs = qkv.shape[1] // (3 * 128)
    part = lambda which: pl.BlockSpec((seq, 128), lambda s, p: (s, which * pairs + p))
    return pl.pallas_call(
        attend_forward,
        grid=(rows // seq, pairs),
        in_specs=[part(0), part(1), part(2), pl.BlockSpec((1, seq, 1), lambda s, p: (s, 0, 0))],
        out_specs=[part(0), pl.BlockSpec((1, 1, 2, seq), lambda s, p: (s, p, 0, 0))],
        out_shape=[
            jax.ShapeDtypeStruct((rows, pairs * 128), BF16),
            jax.ShapeDtypeStruct((rows // seq, pairs, 2, seq), F32),
        ],
        compiler_params=pltpu.CompilerParams(vmem_limit_bytes=40 << 20),
        cost_estimate=pl.CostEstimate(
            flops=rows * pairs * 2 * seq * 256 * 2 * 2, bytes_accessed=4 << 20, transcendentals=0
        ),
        name="attend_forward",
    )(qkv, qkv, qkv, labels)


def attend_backward(
    q_ref, k_ref, v_ref, out_ref, grad_ref, lab_ref, log_ref, dq_ref, dk_ref, dv_ref
):
    labels = lab_ref[0]
    shape = (labels.shape[0], 128)
    low = lax.broadcasted_iota(jnp.int32, shape, 1) < HEAD_DIM
    q_extra, k_extra = query_marks(labels, shape), key_marks(labels, shape)
    q = q_ref[...] * jnp.asarray(0.125, BF16)
    k, v, grad = k_ref[...], v_ref[...], grad_ref[...]
    zero = jnp.zeros_like(q)
    inner = (grad.astype(F32) * out_ref[...].astype(F32)).T
    dqs, dks, dvs = [], [], []
    for t in range(2):
        mine = low if t == 0 else jnp.logical_not(low)
        half = slice(t * HEAD_DIM, (t + 1) * HEAD_DIM)
        scores = dims(jnp.where(mine, k, k_extra), jnp.where(mine, q, q_extra), 1, 1)
        soft = jnp.exp(scores - log_ref[0, 0, t : t + 1])
        grad_soft = dims(v, jnp.where(mine, grad, zero), 1, 1)
        row_inner = jnp.sum(inner[half], axis=0, keepdims=True)
        grad_scores = (soft * (grad_soft - row_inner)).astype(BF16)
        dvs.append(dims(soft.astype(BF16), grad, 1, 0))
        dks.append(dims(grad_scores, q, 1, 0))
        dqs.append(dims(k, grad_scores, 0, 0)[half])
    dv_ref[...] = jnp.where(low, dvs[0], dvs[1]).astype(BF16)
    dk_ref[...] = jnp.where(low, dks[0], dks[1]).astype(BF16)
    dq_ref[...] = (jnp.concatenate(dqs, axis=0).T * 0.125).astype(BF16)


def run_attend_backward(qkv, out, grad, labels, logsum, seq):
    rows = qkv.shape[0]
    pairs = qkv.shape[1] // (3 * 128)
    part = lambda which: pl.BlockSpec((seq, 128), lambda s, p: (s, which * pairs + p))
    shape = jax.ShapeDtypeStruct((rows, pairs * 128), BF16)
    return pl.pallas_call(
        attend_backward,
        grid=(rows // seq, pairs),
        in_specs=[
            part(0),
            part(1),
            part(2),
            part(0),
            part(0),
            pl.BlockSpec((1, seq, 1), lambda s, p: (s, 0, 0)),
            pl.BlockSpec((1, 1, 2, seq), lambda s, p: (s, p, 0, 0)),
        ],
        out_specs=[part(0)] * 3,
        out_shape=[shape] * 3,
        compiler_params=pltpu.CompilerParams(vmem_limit_bytes=40 << 20),
        cost_estimate=pl.CostEstimate(
            flops=rows * pairs * 2 * seq * 256 * 2 * 3, bytes_accessed=8 << 20, transcendentals=0
        ),
        name="attend_backward",
    )(qkv, qkv, qkv, out, grad, labels, logsum)


def gelu_pair(inner):
    t = 1.0 / (1.0 + (0.3275911 * 0.7071067811865476) * jnp.abs(inner))
    bell = jnp.exp(-0.5 * (inner * inner))
    poly = 0.7107068705 + t * (-0.7265760135 + t * 0.5307027145)
    tail = t * (0.127414796 + t * (-0.142248368 + t * poly)) * bell
    phi = jnp.where(inner >= 0, 1.0 - tail, tail)
    return inner * phi, phi + inner * (bell * 0.3989422804014327)


def norm_parts(values):
    centered = values - jnp.mean(values, axis=-1, keepdims=True)
    factor = lax.rsqrt(jnp.mean(centered * centered, axis=-1, keepdims=True) + NORM_EPS)
    return centered * factor, factor


def norm_back(grad_out, normed, factor, gain):
    scaled = grad_out * gain
    return factor * (
        scaled
        - jnp.mean(scaled, axis=-1, keepdims=True)
        - normed * jnp.mean(scaled * normed, axis=-1, keepdims=True)
    )


def feed_forward(
    chunk,
    ctx_a,
    ctx_b,
    tokens,
    w_out,
    w_up,
    w_down,
    vectors,
    b_up,
    cotangent,
    live,
    y_ref,
    hidden_ref,
    normed_ref,
    factor_ref,
    act_ref,
    slope_ref,
    mid_ref,
    sums_ref,
):
    b_out, gain_one, shift_one, b_down, gain_two, shift_two = [
        vectors[i : i + 1] for i in range(6)
    ]
    context = jnp.concatenate([ctx_a[...], ctx_b[...]], axis=1)
    normed_one, factor_one = norm_parts(
        tokens[...].astype(F32) + matmul(context, w_out[...]) + b_out
    )
    normed_ref[...] = normed_one
    factor_ref[...] = factor_one
    hidden = normed_one * gain_one + shift_one
    hidden_low = hidden.astype(BF16)
    hidden_ref[...] = hidden_low
    total = hidden + b_down
    for j in range(w_up.shape[1] // chunk):
        cols = slice(j * chunk, (j + 1) * chunk)
        activated, slope = gelu_pair(matmul(hidden_low, w_up[:, cols]) + b_up[:, cols])
        activated = activated.astype(BF16)
        act_ref[:, cols] = activated
        slope_ref[:, cols] = slope.astype(BF16)
        total = total + matmul(activated, w_down[cols, :])
    normed_two, factor_two = norm_parts(total)
    y_ref[...] = (normed_two * gain_two + shift_two).astype(BF16)
    grad_y = cotangent[...].astype(F32) * live[...]
    grad_mid = norm_back(grad_y, normed_two, factor_two, gain_two)
    mid_ref[...] = grad_mid

    @pl.when(pl.program_id(0) == 0)
    def _():
        sums_ref[...] = jnp.zeros_like(sums_ref)

    sums_ref[0:1] += jnp.sum(grad_y * normed_two, axis=0, keepdims=True)
    sums_ref[1:2] += jnp.sum(grad_y, axis=0, keepdims=True)
    sums_ref[2:3] += jnp.sum(grad_mid, axis=0, keepdims=True)


def run_feed_forward(
    ctx_a, ctx_b, tokens, w_out, w_up, w_down, vectors, b_up, cotangent, live, block=256, chunk=512
):
    rows, width = tokens.shape
    ff = w_up.shape[1]
    half = ctx_a.shape[1]
    token = lambda cols: pl.BlockSpec((block, cols), lambda i: (i, 0))
    held = lambda shape: pl.BlockSpec(shape, lambda i: (0, 0), pipeline_mode=pl.Buffered(1))
    out = jax.ShapeDtypeStruct
    return pl.pallas_call(
        functools.partial(feed_forward, chunk),
        grid=(rows // block,),
        in_specs=[
            token(half),
            token(half),
            token(width),
            held(w_out.shape),
            held(w_up.shape),
            held(w_down.shape),
            held(vectors.shape),
            held(b_up.shape),
            token(width),
            token(1),
        ],
        out_specs=[
            token(width),
            token(width),
            token(width),
            token(1),
            token(ff),
            token(ff),
            token(width),
            pl.BlockSpec((8, width), lambda i: (0, 0)),
        ],
        out_shape=[
            out((rows, width), BF16),
            out((rows, width), BF16),
            out((rows, width), F32),
            out((rows, 1), F32),
            out((rows, ff), BF16),
            out((rows, ff), BF16),
            out((rows, width), F32),
            out((8, width), F32),
        ],
        compiler_params=pltpu.CompilerParams(vmem_limit_bytes=56 << 20),
        cost_estimate=pl.CostEstimate(
            flops=4 * rows * width * (width + 2 * ff), bytes_accessed=30 << 20, transcendentals=0
        ),
        name="feed_forward",
    )(ctx_a, ctx_b, tokens, w_out, w_up, w_down, vectors, b_up, cotangent, live)


def feed_backward(
    groups,
    group_rows,
    core_ref,
    act,
    slope,
    mid,
    w_down,
    w_up,
    hidden,
    ctx_a,
    ctx_b,
    w_out,
    normed,
    factor,
    gain_one,
    down_keep,
    down_send,
    up_keep,
    up_send,
    b_up_ref,
    first_ref,
    grad_ctx_a,
    grad_ctx_b,
    w_out_ref,
    sums_ref,
    mid_low,
    grad_hidden,
):
    step = pl.program_id(0)
    core = core_ref[0]

    @pl.when(step == 0)
    def _():
        grad_mid = mid[...]
        mid_low[...] = grad_mid.astype(BF16)
        grad_hidden[...] = grad_mid

    def put(result, keep, send):
        result = result.reshape(groups, 2, group_rows, result.shape[-1])
        keep[...] = jnp.where(core == 0, result[:, 0], result[:, 1]).astype(BF16)
        send[...] = jnp.where(core == 0, result[:, 1], result[:, 0]).astype(BF16)

    put(dims(act[...], mid_low[...], 0, 0), down_keep, down_send)
    grad_inner = dims(mid_low[...], w_down[...], 1, 1) * slope[...].astype(F32)
    grad_inner = grad_inner.astype(BF16)
    b_up_ref[...] = jnp.sum(grad_inner.astype(F32), axis=0, keepdims=True)
    put(dims(grad_inner, hidden[...], 0, 0), up_keep, up_send)
    grad_hidden[...] += dims(grad_inner, w_up[...], 1, 1)

    @pl.when(step == pl.num_programs(0) - 1)
    def _():
        grad, normed_one = grad_hidden[...], normed[...]
        grad_first = norm_back(grad, normed_one, factor[...], gain_one[...])
        first_ref[...] = grad_first
        sums_ref[0:1] = jnp.sum(grad * normed_one, axis=0, keepdims=True)
        sums_ref[1:2] = jnp.sum(grad, axis=0, keepdims=True)
        sums_ref[2:3] = jnp.sum(grad_first, axis=0, keepdims=True)
        first_low = grad_first.astype(BF16)
        grad_ctx = dims(first_low, w_out[...], 1, 1).astype(BF16)
        half = grad_ctx_a.shape[1]
        grad_ctx_a[...] = grad_ctx[:, :half]
        grad_ctx_b[...] = grad_ctx[:, half:]
        w_out_ref[:half] = dims(ctx_a[...], first_low, 0, 0).astype(BF16)
        w_out_ref[half:] = dims(ctx_b[...], first_low, 0, 0).astype(BF16)


def run_feed_backward(
    core,
    act,
    slope,
    mid,
    w_down,
    w_up,
    hidden,
    ctx_a,
    ctx_b,
    w_out,
    normed,
    factor,
    gain_one,
    rows_dev,
    block=384,
):
    rows, width = mid.shape
    ff = w_up.shape[1]
    half = ctx_a.shape[1]
    group_rows = 2 * rows_dev
    groups = block // (2 * group_rows)
    held = lambda shape: pl.BlockSpec(shape, lambda i, c: (0, 0), pipeline_mode=pl.Buffered(1))
    columns = pl.BlockSpec((rows, block), lambda i, c: (0, i))
    pieces = pl.BlockSpec((groups, group_rows, width), lambda i, c: (i, 0, 0))
    out = jax.ShapeDtypeStruct
    piece_shape = out((ff // (2 * group_rows), group_rows, width), BF16)
    return pl.pallas_call(
        functools.partial(feed_backward, groups, group_rows),
        grid_spec=pltpu.PrefetchScalarGridSpec(
            num_scalar_prefetch=1,
            grid=(ff // block,),
            in_specs=[
                columns,
                columns,
                held((rows, width)),
                pl.BlockSpec((block, width), lambda i, c: (i, 0)),
                pl.BlockSpec((width, block), lambda i, c: (0, i)),
                held((rows, width)),
                held((rows, half)),
                held((rows, half)),
                held((width, width)),
                held((rows, width)),
                held((rows, 1)),
                held((1, width)),
            ],
            out_specs=[
                pieces,
                pieces,
                pieces,
                pieces,
                pl.BlockSpec((1, block), lambda i, c: (0, i)),
                held((rows, width)),
                held((rows, half)),
                held((rows, half)),
                held((width, width)),
                held((8, width)),
            ],
            scratch_shapes=[pltpu.VMEM((rows, width), BF16), pltpu.VMEM((rows, width), F32)],
        ),
        out_shape=[
            piece_shape,
            piece_shape,
            piece_shape,
            piece_shape,
            out((1, ff), F32),
            out((rows, width), F32),
            out((rows, half), BF16),
            out((rows, half), BF16),
            out((width, width), BF16),
            out((8, width), F32),
        ],
        compiler_params=pltpu.CompilerParams(vmem_limit_bytes=56 << 20),
        cost_estimate=pl.CostEstimate(
            flops=2 * rows * width * (4 * ff + 2 * width), bytes_accessed=50 << 20, transcendentals=0
        ),
        name="feed_backward",
    )(
        core, act, slope, mid, w_down, w_up, hidden, ctx_a, ctx_b, w_out, normed, factor, gain_one
    )


class Cube:
    def __init__(self, mesh):
        self.n_dp, self.n_head = mesh.shape["dp"], mesh.shape["head"]
        self.size = self.n_dp * self.n_head
        self.n_bits = self.size.bit_length() - 1
        self.index = lax.axis_index("dp") * self.n_head + lax.axis_index("head")

    def bit(self, which):
        return (self.index >> which) & 1

    def swap(self, value, which):
        pairs = [(i, i ^ (1 << which)) for i in range(self.size)]
        return lax.ppermute(value, AXES, pairs)

    def halve(self, value, axis, which):
        mine = self.bit(which)
        send = lax.dynamic_index_in_dim(value, 1 - mine, axis, keepdims=False)
        keep = lax.dynamic_index_in_dim(value, mine, axis, keepdims=False)
        return keep + self.swap(send, which)

    def double(self, value, which):
        value = lax.optimization_barrier(value)
        return value + self.swap(value, which)

    def join(self, value, which):
        other = self.swap(value, which)
        first = self.bit(which) == 0
        return jnp.concatenate(
            [jnp.where(first, value, other), jnp.where(first, other, value)], axis=0
        )

    def scatter_pieces(self, keep, send, order, rows_dev):
        value = keep + self.swap(send, 1)
        bits = list(range(self.n_bits - 1, 1, -1)) + [0]
        value = value.reshape((2,) * len(bits) + (rows_dev, value.shape[-1]))
        for which in order:
            value = self.halve(value, bits.index(which), which)
            bits.remove(which)
        return value

    def reduce_rows(self, value, order):
        halved = []
        for which in order:
            rows = value.shape[0]
            if rows % 32 == 0:
                value = self.halve(value.reshape(2, rows // 2, value.shape[1]), 0, which)
                halved.append(which)
            else:
                value = self.double(value, which)
        return value, halved

    def gather_rows(self, value, halved):
        for which in reversed(halved):
            value = self.join(value, which)
        return value


def shards(
    mesh,
    tokens,
    labels,
    micro_counts,
    w_query,
    b_query,
    w_key,
    w_value,
    b_value,
    w_out,
    b_out,
    gain_one,
    shift_one,
    w_up,
    b_up,
    w_down,
    b_down,
    gain_two,
    shift_two,
    cotangent,
):
    cube = Cube(mesh)
    rows, width = tokens.shape
    seq = labels.shape[1]
    half = w_query.shape[1]
    ff = w_up.shape[1]
    head, core = cube.bit(0), cube.bit(1)
    upper = list(range(2, cube.n_bits))

    own_w = jnp.concatenate([w_query, w_key, w_value], axis=1)
    part = lax.dynamic_index_in_dim(own_w.reshape(2, width // 2, 3 * half), core, 0, False)
    peer_w = cube.join(cube.swap(part, 0), 1)
    own_b = jnp.concatenate([b_query, jnp.zeros_like(b_query), b_value])
    peer_b = cube.swap(own_b, 0)
    own_rows = lax.dynamic_slice_in_dim(w_out, head * half, half, 0)
    peer_rows = lax.dynamic_slice_in_dim(w_out, (1 - head) * half, half, 0)
    w_out_turned = jnp.concatenate([own_rows, peer_rows], axis=0)
    n_seq = rows // seq
    marks = lax.dynamic_slice_in_dim(labels, head * n_seq, n_seq, 0)[:, :, None]
    position = jnp.arange(rows, dtype=jnp.int32) % seq
    live = (position // (seq // MICRO) < micro_counts[0]).astype(F32)[:, None]
    vectors = jnp.stack(
        [b_out, gain_one, shift_one, b_down, gain_two, shift_two, b_down, b_down]
    )

    def project(weight, offset):
        return (matmul(tokens, weight) + offset.astype(F32)).astype(BF16)

    own_qkv = project(own_w, own_b)
    own_ctx, own_log = run_attend_forward(own_qkv, marks, seq)
    peer_qkv = project(peer_w, peer_b)
    peer_ctx, peer_log = run_attend_forward(peer_qkv, marks, seq)

    layer_output, hidden_low, normed_one, factor_one, activated, slope, grad_mid, sums_two = (
        run_feed_forward(
            own_ctx,
            peer_ctx,
            tokens,
            w_out_turned,
            w_up,
            w_down,
            vectors,
            b_up[None],
            cotangent,
            live,
        )
    )
    rows_dev = ff // cube.size
    (
        down_keep,
        down_send,
        up_keep,
        up_send,
        grad_b_up,
        grad_first,
        own_grad_ctx,
        peer_grad_ctx,
        out_local,
        sums_one,
    ) = run_feed_backward(
        core[None],
        activated,
        slope,
        grad_mid,
        w_down,
        w_up,
        hidden_low,
        own_ctx,
        peer_ctx,
        w_out_turned,
        normed_one,
        factor_one,
        gain_one[None],
        rows_dev,
    )
    down_slice = cube.scatter_pieces(down_keep, down_send, [0] + upper, rows_dev)
    up_slice = cube.scatter_pieces(up_keep, up_send, [2, 0] + upper[1:], rows_dev)
    grad_w_down = down_slice.astype(F32)
    grad_w_up = up_slice.astype(F32).T

    small = jnp.concatenate(
        [sums_one[:3], sums_two[:3], grad_b_up.reshape(ff // width, width)], axis=0
    )
    for which in [1, 0] + upper:
        small = cube.double(small, which)

    out_own = out_local[:half] + cube.swap(out_local[half:], 0)
    out_own, halved = cube.reduce_rows(out_own, [1] + upper)
    out_own = cube.gather_rows(out_own, halved)
    out_peer = cube.swap(out_own, 0)
    grad_w_out = jnp.concatenate(
        [jnp.where(head == 0, out_own, out_peer), jnp.where(head == 0, out_peer, out_own)], axis=0
    ).astype(F32)

    def backward(qkv, ctx, grad_ctx, logsum):
        grads = run_attend_backward(qkv, ctx, grad_ctx, marks, logsum, seq)
        bias = jnp.stack([jnp.sum(grads[0].astype(F32), 0), jnp.sum(grads[2].astype(F32), 0)])
        grads = jnp.concatenate(grads, axis=1)
        return grads, bias, dims(tokens, grads, 0, 0).astype(BF16)

    peer_grads, peer_bias, peer_local = backward(peer_qkv, peer_ctx, peer_grad_ctx, peer_log)
    own_grads, own_bias, own_local = backward(own_qkv, own_ctx, own_grad_ctx, own_log)
    from_peer = cube.halve(peer_local.reshape(2, width // 2, 3 * half), 0, 1)
    own_sum = cube.halve(own_local.reshape(2, width // 2, 3 * half), 0, 1)
    own_sum = own_sum + cube.swap(from_peer, 0)
    own_sum, halved = cube.reduce_rows(own_sum, upper)
    own_sum = cube.gather_rows(own_sum, [1] + halved).astype(F32)
    grad_w_query, grad_w_key, grad_w_value = jnp.split(own_sum, 3, axis=1)
    bias = own_bias + cube.swap(peer_bias, 0)
    for which in [1] + upper:
        bias = cube.double(bias, which)

    grad_tokens = grad_first + dims(own_grads, own_w, 1, 1) + dims(peer_grads, peer_w, 1, 1)
    return (
        layer_output,
        grad_tokens,
        grad_w_query,
        bias[0],
        grad_w_key,
        grad_w_value,
        bias[1],
        grad_w_out,
        small[2],
        small[0],
        small[1],
        grad_w_up,
        small[6:].reshape(ff),
        grad_w_down,
        small[5],
        small[3],
        small[4],
    )


def solution(mesh):
    rows = P(("dp", "head"), None)
    placed = (rows, P("dp", None), P("dp"), P(None, "head"), P("head"), P(None, "head"))
    placed += (P(None, "head"), P("head")) + (P(),) * 10 + (rows,)
    columns = P(None, "head")
    out_specs = (rows, rows, columns, P("head"), columns, columns, P("head"))
    out_specs += (P(),) * 4 + (P(None, ("dp", "head")), P(), rows, P(), P(), P())
    return jax.shard_map(
        functools.partial(shards, mesh),
        mesh=mesh,
        in_specs=placed,
        out_specs=out_specs,
        check_vma=False,
    )
```

time: 1010 us -> 330 us (0.33)
  waiting for transfers between devices: 537 us -> 116 us
  matrix products: 226 us -> 20.2 us
  Pallas kernels: 0 us -> 112 us
  blocking collectives: 95.3 us -> 0 us
  local copies, waits for them, and re-layouts: 86.2 us -> 22 us
  starting transfers between devices: 5.41 us -> 36.6 us
  other arithmetic: 33.3 us -> 17.6 us
  between operations: 15.5 us -> 2.61 us
    reduce_scatter x3 -> x0, waiting for transfers between devices: 340 us -> none  [the longest x1 142 us: shards(): lax.psum_scatter(down_turned, ('dp', 'head'), scatter_dimension=1, tiled=...]
    dot_general x46 -> x6, matrix products: 226 us -> 20.2 us  [the longest x4 13.7 us: dims(): lax.dot_general(left, right, (((left_dim,), (right_dim,)), ((), ())), pre...]
    psum x2 -> x0, waiting for transfers between devices: 133 us -> none  [the longest x1 133 us: shards(): lax.psum((out_local, grad_b_out, grad_gain_one, grad_shift_one, grad_b_up...]
    ppermute x0 -> x42, waiting for transfers between devices: none -> 116 us  [swap(): return lax.ppermute(value, AXES, pairs)]
    pallas_call x0 -> x6, Pallas kernels: none -> 112 us  [the longest x1 38.2 us: run_feed_backward(): pl.pallas_call(functools.partial(feed_backward, groups, group_rows), grid...]
    psum x2 -> x0, blocking collectives: 74 us -> none  [the longest x1 40.9 us: shards(): lax.psum((out_local, grad_b_out, grad_gain_one, grad_shift_one, grad_b_up...]
    all_gather x1 -> x0, waiting for transfers between devices: 47.9 us -> none  [shards(): attend_in = lax.all_gather(tokens, 'head', axis=0, tiled=True)]
    ppermute x0 -> x42, starting transfers between devices: none -> 36.6 us  [swap(): return lax.ppermute(value, AXES, pairs)]
  transfers between devices with their start and end apart: 7 -> 42, of which waited for: 6 -> 19; matrix products, arithmetic and copies ran while one was open for 6% -> 11% of each run, Pallas kernels for 0% -> 3%
where the time goes in v1:
time: 330 us; the launch traced here: 327 us
  waiting for transfers between devices  116 us (35%)
  Pallas kernels  112 us (34%)
  starting transfers between devices  36.6 us (11%)
  local copies, waits for them, and re-layouts  22 us (7%)
  matrix products  20.2 us (6%)
  other arithmetic  17.6 us (5%)
    ppermute x42, waiting for transfers between devices, swap(): return lax.ppermute(value, AXES, pairs)  116 us
    pallas_call x1, Pallas kernels, run_feed_backward(): pl.pallas_call(functools.partial(feed_backward, groups, group_rows), grid...  38.2 us
    ppermute x42, starting transfers between devices, swap(): return lax.ppermute(value, AXES, pairs)  36.6 us
    pallas_call x1, Pallas kernels, run_feed_forward(): pl.pallas_call(functools.partial(feed_forward, chunk), grid=(rows // bloc...  33.2 us
    pallas_call x2, Pallas kernels, run_attend_backward(): pl.pallas_call(attend_backward, grid=(rows // seq, pairs), in_specs=[part...  22.3 us
    pallas_call x2, Pallas kernels, run_attend_forward(): pl.pallas_call(attend_forward, grid=(rows // seq, pairs), in_specs=[part(...  18.5 us
    dot_general x4, matrix products, dims(): lax.dot_general(left, right, (((left_dim,), (right_dim,)), ((), ())), pre...  13.7 us
    unnamed x90, local copies, waits for them, and re-layouts  11.4 us
  transfers between devices with their start and end apart: 42, of which 19 were waited for; matrix products, arithmetic and copies ran while one was open for 11% of the time, Pallas kernels for 3%

profile of v1, /device:TPU:0, one launch (start us, length us, event | category | flops | bytes accessed | tf_op | source)
XLA Modules:
  0.0 327.0 jit_solution(1641721669363921660)
XLA Ops:
  4.2 2.9 collective-permute-start
  9.9 17.2 %collective-permute-done = bf16[384,1152]{1,0:T(8,128)(2,1)} collective-permute-done((bf16[384,1152]{1,0:T(8,128)(2,1)}, bf16[384,1152]{1,0:T(8,128)(2,1)}, u32[]{:S(2)}, u32[]{:S(2)}) %collective-permute-start) | collective-permute-done | bytes 884768 | tf_op jit(solution)/shard_map/ppermute | solution.py:428
  27.4 4.3 %fusion.q_ref.k_ref.v_ref = bf16[1024,1152]{1,0:T(8,128)(2,1)S(1)} fusion(bf16[1024,768]{1,0:T(8,128)(2,1)} %tokens.1, bf16[768,1152]{1,0:T(8,128)(2,1)} %copy-done.14, f32[1152]{0:T(1024)S(1)} %get-tuple-element.109), kind=kOutput, calls=%fused_computation.4 | convolution fusion | flops 1814298624 | bytes 5706240 | tf_op jit(solution)/shard_map/dot_general | solution.py:26
  31.8 9.3 %attend_forward.2 = (bf16[1024,384]{1,0:T(8,128)(2,1)S(1)}, f32[2,3,2,512]{3,2,1,0:T(2,128)S(1)}) custom-call(bf16[1024,1152]{1,0:T(8,128)(2,1)S(1)} %fusion.q_ref.k_ref.v_ref, bf16[1024,1152]{1,0:T(8,128)(2,1)S(1)} %fusion.q_ref.k_ref.v_ref, bf16[1024,1152]{1,0:T(8,128)(2,1)S(1)} %fusion.q_ref.k_ref.v_ref, s32[2,512,1]{2,1,0:T(8,128)S(1)} %copy.39.lab_ref), custom_call_target="tpu_custom_call" | custom-call | flops 3221225472 | bytes 4194304 | tf_op jit(solution)/shard_map/attend_forward/pallas_call | solution.py:63
  41.2 1.4 copy-done.4
  44.3 1.7 broadcast_select_fusion.3
  47.2 2.2 fusion.1.q_ref.k_ref.v_ref
  49.4 9.2 %attend_forward.3 = (bf16[1024,384]{1,0:T(8,128)(2,1)S(1)}, f32[2,3,2,512]{3,2,1,0:T(2,128)S(1)}) custom-call(bf16[1024,1152]{1,0:T(8,128)(2,1)S(1)} %fusion.1.q_ref.k_ref.v_ref, bf16[1024,1152]{1,0:T(8,128)(2,1)S(1)} %fusion.1.q_ref.k_ref.v_ref, bf16[1024,1152]{1,0:T(8,128)(2,1)S(1)} %fusion.1.q_ref.k_ref.v_ref, s32[2,512,1]{2,1,0:T(8,128)S(1)} %copy.39.lab_ref), custom_call_target="tpu_custom_call" | custom-call | flops 3221225472 | bytes 4194304 | tf_op jit(solution)/shard_map/attend_forward/pallas_call | solution.py:63
  59.5 33.2 %feed_forward.1 = (bf16[1024,768]{1,0:T(8,128)(2,1)}, bf16[1024,768]{1,0:T(8,128)(2,1)}, f32[1024,768]{1,0:T(8,128)}, f32[1024,1]{1,0:T(8,128)}, bf16[1024,3072]...) custom-call(bf16[1024,384]{1,0:T(8,128)(2,1)} %copy-done.6, ...), custom_call_target="tpu_custom_call" | custom-call | flops 21743271936 | bytes 31457280 | tf_op jit(solution)/shard_map/feed_forward/pallas_call | solution.py:224
  92.7 38.2 %feed_backward.1 = (bf16[8,192,768]{2,1,0:T(8,128)(2,1)}, bf16[8,192,768]{2,1,0:T(8,128)(2,1)}, bf16[8,192,768]{2,1,0:T(8,128)(2,1)}, bf16[8,192,768]{2,1,0:T(8,...) custom-call(s32[1]{0:T(128)} %bitcast.7.core_ref, ...), custom_call_target="tpu_custom_call" | custom-call | flops 21743271936 | bytes 52428800 | tf_op jit(solution)/shard_map/feed_backward/pallas_call | solution.py:361
  132.0 11.1 %attend_backward.2 = (bf16[1024,384]{1,0:T(8,128)(2,1)S(1)}, bf16[1024,384]{1,0:T(8,128)(2,1)S(1)}, bf16[1024,384]{1,0:T(8,128)(2,1)S(1)}) custom-call(bf16[1024,1152]{1,0:T(8,128)(2,1)S(1)} %copy-done.5, bf16[1024,1152]{1,0:T(8,128)(2,1)S(1)} %copy-done.5, bf16[1024,1152]{1,0:T(8,128)(2,1)S(1)} %copy-done.5, bf16[1024,384]{1,0:T(8,128)(2,1)S(1)} %copy-done.7, ...), custom_call_target="tpu_custom_call" | custom-call | flops 4831838208 | bytes 8388608 | tf_op jit(solution)/shard_map/attend_backward/pallas_call | solution.py:113
  144.7 3.9 %fusion.17 = f32[1024,768]{1,0:T(8,128)} fusion(bf16[1024,1152]{1,0:T(8,128)(2,1)S(1)} %constant_dynamic-update-slice_fusion.3, bf16[768,1152]{1,0:T(8,128)(2,1)S(1)} %copy-done.15), kind=kOutput, calls=%fused_computation.124 | convolution fusion | flops 1811939328 | bytes 7274496 | tf_op jit(solution)/shard_map/dot_general | solution.py:20
  148.6 3.5 %convolution_convert_fusion.1 = bf16[1152,768]{0,1:T(8,128)(2,1)} fusion(bf16[1024,1152]{1,0:T(8,128)(2,1)S(1)} %constant_dynamic-update-slice_fusion.3, bf16[1024,768]{1,0:T(8,128)(2,1)S(1)} %copy-done.38), kind=kOutput, calls=%fused_computation.3 | convolution fusion | flops 1812824064 | bytes 5701632 | tf_op jit(solution)/shard_map/dot_general | solution.py:20
  152.1 11.3 %attend_backward.3 = (bf16[1024,384]{1,0:T(8,128)(2,1)S(1)}, bf16[1024,384]{1,0:T(8,128)(2,1)S(1)}, bf16[1024,384]{1,0:T(8,128)(2,1)S(1)}) custom-call(bf16[1024,1152]{1,0:T(8,128)(2,1)S(1)} %fusion.1.q_ref.k_ref.v_ref, bf16[1024,1152]{1,0:T(8,128)(2,1)S(1)} %fusion.1.q_ref.k_ref.v_ref, bf16[1024,1152]{1,0:T(8,128)(2,1)S(1)} %fusion.1.q_ref.k_ref.v_ref, ...), custom_call_target="tpu_custom_call" | custom-call | flops 4831838208 | bytes 8388608 | tf_op jit(solution)/shard_map/attend_backward/pallas_call | solution.py:113
  164.7 1.8 collective-permute-start.13
  172.0 12.8 %collective-permute-done.18 = bf16[384,768]{1,0:T(8,128)(2,1)S(1)} collective-permute-done((bf16[384,768]{1,0:T(8,128)(2,1)S(1)}, bf16[384,768]{1,0:T(8,128)(2,1)S(1)}, u32[]{:S(2)}, u32[]{:S(2)}) %collective-permute-start.18) | collective-permute-done | bytes 589856 | tf_op jit(solution)/shard_map/ppermute | solution.py:428
  185.0 2.3 convolution_convert_fusion
  187.3 1.6 collective-permute-start.15
  189.7 1.3 collective-permute-done.15
  191.0 1.6 collective-permute-start.16
  195.5 2.6 collective-permute-start.17
  198.2 1.7 collective-permute-start.30
  201.4 2.9 collective-permute-done.21
  204.3 2.3 collective-permute-start.22
  206.6 4.0 %add_add_fusion = f32[1024,768]{1,0:T(8,128)} fusion(f32[1024,768]{1,0:T(8,128)S(1)} %copy-done.40, f32[1024,768]{1,0:T(8,128)S(1)} %copy-done.41, bf16[1024,1152]{1,0:T(8,128)(2,1)S(1)} %copy-done.23, bf16[384,1152]{1,0:T(8,128)(2,1)S(1)} %copy-done.21, bf16[384,1152]{1,0:T(8,128)(2,1)S(1)} %copy-done.19), kind=kOutput, calls=%fused_computation.6 | convolution fusion | flops 1817051136 | bytes 13565952 | tf_op jit(solution)/shard_map/dot_general | solution.py:20
  212.0 1.9 collective-permute-start.23
  213.9 7.9 %collective-permute-done.5 = bf16[384,1152]{1,0:T(8,128)(2,1)S(1)} collective-permute-done((bf16[384,1152]{1,0:T(8,128)(2,1)S(1)}, bf16[384,1152]{1,0:T(8,128)(2,1)S(1)}, u32[]{:S(2)}, u32[]{:S(2)}) %collective-permute-start.5) | collective-permute-done | bytes 884768 | tf_op jit(solution)/shard_map/ppermute | solution.py:428
  224.7 9.3 %collective-permute-done.6 = bf16[192,1152]{1,0:T(8,128)(2,1)S(1)} collective-permute-done((bf16[192,1152]{1,0:T(8,128)(2,1)S(1)}, bf16[192,1152]{1,0:T(8,128)(2,1)S(1)}, u32[]{:S(2)}, u32[]{:S(2)}) %collective-permute-start.6) | collective-permute-done | bytes 442400 | tf_op jit(solution)/shard_map/ppermute | solution.py:428
  234.1 1.9 collective-permute-start.7
  236.1 5.2 %collective-permute-done.7 = bf16[96,1152]{1,0:T(8,128)(2,1)S(1)} collective-permute-done((bf16[96,1152]{1,0:T(8,128)(2,1)S(1)}, bf16[96,1152]{1,0:T(8,128)(2,1)S(1)}, u32[]{:S(2)}, u32[]{:S(2)}) %collective-permute-start.7) | collective-permute-done | bytes 221216 | tf_op jit(solution)/shard_map/ppermute | solution.py:428
  241.6 9.1 %collective-permute-done.8 = bf16[48,1152]{1,0:T(8,128)(2,1)S(1)} collective-permute-done((bf16[48,1152]{1,0:T(8,128)(2,1)S(1)}, bf16[48,1152]{1,0:T(8,128)(2,1)S(1)}, u32[]{:S(2)}, u32[]{:S(2)}) %collective-permute-start.8) | collective-permute-done | bytes 110624 | tf_op jit(solution)/shard_map/ppermute | solution.py:428
  250.8 5.8 %collective-permute-done.9 = bf16[48,1152]{1,0:T(8,128)(2,1)S(1)} collective-permute-done((bf16[48,1152]{1,0:T(8,128)(2,1)S(1)}, bf16[48,1152]{1,0:T(8,128)(2,1)S(1)}, u32[]{:S(2)}, u32[]{:S(2)}) %collective-permute-start.9) | collective-permute-done | bytes 110624 | tf_op jit(solution)/shard_map/ppermute | solution.py:428
  260.3 2.4 collective-permute-done.10
  265.1 2.9 add.267
  268.9 1.5 collective-permute-done.26
  270.4 1.3 broadcast_select_fusion.5
  271.7 19.8 %collective-permute-done.11 = bf16[192,1152]{1,0:T(8,128)(2,1)} collective-permute-done((bf16[192,1152]{1,0:T(8,128)(2,1)}, bf16[192,1152]{1,0:T(8,128)(2,1)}, u32[]{:S(2)}, u32[]{:S(2)}) %collective-permute-start.11) | collective-permute-done | bytes 442400 | tf_op jit(solution)/shard_map/ppermute | solution.py:428
  292.9 2.0 collective-permute-start.34
  294.9 2.4 collective-permute-done.38
  298.1 1.6 maximum_convert_fusion.1
  299.6 6.0 %collective-permute-done.34 = bf16[2,2,96,768]{3,2,1,0:T(8,128)(2,1)S(1)} collective-permute-done((bf16[2,2,96,768]{3,2,1,0:T(8,128)(2,1)S(1)}, bf16[2,2,96,768]{3,2,1,0:T(8,128)(2,1)S(1)}, u32[]{:S(2)}, u32[]{:S(2)}) %collective-permute-start.34) | collective-permute-done | bytes 589856 | tf_op jit(solution)/shard_map/ppermute | solution.py:428
  305.7 2.1 collective-permute-start.35
  307.9 1.7 collective-permute-start.40
  310.2 1.9 fusion.16
  312.1 3.4 %collective-permute-done.35 = bf16[2,96,768]{2,1,0:T(8,128)(2,1)S(1)} collective-permute-done((bf16[2,96,768]{2,1,0:T(8,128)(2,1)S(1)}, bf16[2,96,768]{2,1,0:T(8,128)(2,1)S(1)}, u32[]{:S(2)}, u32[]{:S(2)}) %collective-permute-start.35) | collective-permute-done | bytes 294944 | tf_op jit(solution)/shard_map/ppermute | solution.py:428
  315.9 4.0 %collective-permute-done.40 = bf16[2,96,768]{2,1,0:T(8,128)(2,1)S(1)} collective-permute-done((bf16[2,96,768]{2,1,0:T(8,128)(2,1)S(1)}, bf16[2,96,768]{2,1,0:T(8,128)(2,1)S(1)}, u32[]{:S(2)}, u32[]{:S(2)}) %collective-permute-start.40) | collective-permute-done | bytes 294944 | tf_op jit(solution)/shard_map/ppermute | solution.py:428
  320.9 2.5 collective-permute-done.36
  324.2 1.9 collective-permute-done.41
  (241 shorter events, 41.8 us)
Async XLA Ops:
  0.7 26.5 %copy-start = (s32[4,512]{1,0:T(4,128)S(1)}, s32[4,512]{1,0:T(4,128)}, u32[]{:S(2)}) copy-start(s32[4,512]{1,0:T(4,128)} %param.20) | copy-start | bytes 24580
  3.2 24.0 %copy-start.14 = (bf16[768,1152]{1,0:T(8,128)(2,1)}, bf16[768,1152]{1,0:T(8,128)(2,1)S(1)}, u32[]{:S(2)}) copy-start(bf16[768,1152]{1,0:T(8,128)(2,1)S(1)} %constant_dynamic-update-slice_fusion) | copy-start | bytes 5308420
  4.2 22.9 %collective-permute-start = (bf16[384,1152]{1,0:T(8,128)(2,1)}, bf16[384,1152]{1,0:T(8,128)(2,1)}, u32[]{:S(2)}, u32[]{:S(2)}) collective-permute-start(bf16[384,1152]{1,0:T(8,128)(2,1)} %dynamic-slice_bitcast_fusion.2), channel_id=1, source_target_pairs={{0,1},{1,0},{2,3},{3,2},{4,5},{5,4},{6,7},{7,6},{8,9},{9,8},{10,11... | collective-permute-start | bytes 2654216 | tf_op jit(solution)/shard_map/ppermute | solution.py:428
  7.2 37.1 %collective-permute-start.2 = (bf16[1152]{0:T(1024)(128)(2,1)S(1)}, bf16[1152]{0:T(1024)(128)(2,1)S(1)}, u32[]{:S(2)}, u32[]{:S(2)}) collective-permute-start(bf16[1152]{0:T(1024)(128)(2,1)S(1)} %get-tuple-element.108), channel_id=1, source_target_pairs={{0,1},{1,0},{2,3},{3,2},{4,5},{5,4},{6,7},{7,6},{8,9},{9,8},{10,11... | collective-permute-start | bytes 6920 | tf_op jit(solution)/shard_map/ppermute | solution.py:428
  27.1 17.1 %collective-permute-start.1 = (bf16[384,1152]{1,0:T(8,128)(2,1)}, bf16[384,1152]{1,0:T(8,128)(2,1)}, u32[]{:S(2)}, u32[]{:S(2)}) collective-permute-start(bf16[384,1152]{1,0:T(8,128)(2,1)} %collective-permute-done), channel_id=1, source_target_pairs={{0,2},{1,3},{2,0},{3,1},{4,6},{5,7},{6,4},{7,5},{8,10},{9,11},{10,... | collective-permute-start | bytes 2654216 | tf_op jit(solution)/shard_map/ppermute | solution.py:428
  27.4 103.5 %copy-start.2 = (s32[2,512,1]{2,1,0:T(8,128)}, s32[2,512,1]{2,1,0:T(8,128)S(1)}, u32[]{:S(2)}) copy-start(s32[2,512,1]{2,1,0:T(8,128)S(1)} %copy.39.lab_ref) | copy-start | bytes 12292
  92.7 38.2 %copy-start.5 = (bf16[1024,1152]{1,0:T(8,128)(2,1)S(1)}, bf16[1024,1152]{1,0:T(8,128)(2,1)}, u32[]{:S(2)}) copy-start(bf16[1024,1152]{1,0:T(8,128)(2,1)} %copy-done.4) | copy-start | bytes 7077892
  92.7 38.2 %copy-start.7 = (bf16[1024,384]{1,0:T(8,128)(2,1)S(1)}, bf16[1024,384]{1,0:T(8,128)(2,1)}, u32[]{:S(2)}) copy-start(bf16[1024,384]{1,0:T(8,128)(2,1)} %copy-done.6) | copy-start | bytes 2359300
  164.7 7.2 %collective-permute-start.13 = (f32[2,384]{1,0:T(2,128)S(1)}, f32[2,384]{1,0:T(2,128)S(1)}, u32[]{:S(2)}, u32[]{:S(2)}) collective-permute-start(f32[2,384]{1,0:T(2,128)S(1)} %pad_maximum_fusion.12), channel_id=1, source_target_pairs={{0,1},{1,0},{2,3},{3,2},{4,5},{5,4},{6,7},{7,6},{8,9},{9,8},{10,11... | collective-permute-start | bytes 9224 | tf_op jit(solution)/shard_map/ppermute | solution.py:428
  167.8 21.2 %collective-permute-start.27 = (f32[10,768]{1,0:T(8,128)S(1)}, f32[10,768]{1,0:T(8,128)S(1)}, u32[]{:S(2)}, u32[]{:S(2)}) collective-permute-start(f32[10,768]{1,0:T(8,128)S(1)} %pad_maximum_fusion.10), channel_id=1, source_target_pairs={{0,2},{1,3},{2,0},{3,1},{4,6},{5,7},{6,4},{7,5},{8,10},{9,11},{10,... | collective-permute-start | bytes 92168 | tf_op jit(solution)/shard_map/ppermute | solution.py:428
  169.2 15.6 %collective-permute-start.18 = (bf16[384,768]{1,0:T(8,128)(2,1)S(1)}, bf16[384,768]{1,0:T(8,128)(2,1)S(1)}, u32[]{:S(2)}, u32[]{:S(2)}) collective-permute-start(bf16[384,768]{1,0:T(8,128)(2,1)S(1)} %slice.42), channel_id=1, source_target_pairs={{0,1},{1,0},{2,3},{3,2},{4,5},{5,4},{6,7},{7,6},{8,9},{9,8},{10,11... | collective-permute-start | bytes 1769480 | tf_op jit(solution)/shard_map/ppermute | solution.py:428
  171.9 15.5 %collective-permute-start.14 = (f32[2,384]{1,0:T(2,128)S(1)}, f32[2,384]{1,0:T(2,128)S(1)}, u32[]{:S(2)}, u32[]{:S(2)}) collective-permute-start(f32[2,384]{1,0:T(2,128)S(1)} %maximum_add_fusion), channel_id=1, source_target_pairs={{0,2},{1,3},{2,0},{3,1},{4,6},{5,7},{6,4},{7,5},{8,10},{9,11},{10,... | collective-permute-start | bytes 9224 | tf_op jit(solution)/shard_map/ppermute | solution.py:428
  184.9 9.3 %collective-permute-start.19 = (bf16[192,768]{1,0:T(8,128)(2,1)S(1)}, bf16[192,768]{1,0:T(8,128)(2,1)S(1)}, u32[]{:S(2)}, u32[]{:S(2)}) collective-permute-start(bf16[192,768]{1,0:T(8,128)(2,1)S(1)} %dynamic-slice_bitcast_fusion.8), channel_id=1, source_target_pairs={{0,2},{1,3},{2,0},{3,1},{4,6},{5,7},{6,4},{7,5},{8,10},{9,11},{10,... | collective-permute-start | bytes 884744 | tf_op jit(solution)/shard_map/ppermute | solution.py:428
  185.0 21.6 %copy-start.41 = (f32[1024,768]{1,0:T(8,128)S(1)}, f32[1024,768]{1,0:T(8,128)}, u32[]{:S(2)}) copy-start(f32[1024,768]{1,0:T(8,128)} %fusion.17) | copy-start | bytes 9437188
  187.3 3.7 %collective-permute-start.15 = (f32[2,384]{1,0:T(2,128)S(1)}, f32[2,384]{1,0:T(2,128)S(1)}, u32[]{:S(2)}, u32[]{:S(2)}) collective-permute-start(f32[2,384]{1,0:T(2,128)S(1)} %add.246), channel_id=1, source_target_pairs={{0,4},{1,5},{2,6},{3,7},{4,0},{5,1},{6,2},{7,3},{8,12},{9,13},{10,... | collective-permute-start | bytes 9224 | tf_op jit(solution)/shard_map/ppermute | solution.py:428
  188.9 4.2 %collective-permute-start.28 = (f32[10,768]{1,0:T(8,128)S(1)}, f32[10,768]{1,0:T(8,128)S(1)}, u32[]{:S(2)}, u32[]{:S(2)}) collective-permute-start(f32[10,768]{1,0:T(8,128)S(1)} %add.255), channel_id=1, source_target_pairs={{0,1},{1,0},{2,3},{3,2},{4,5},{5,4},{6,7},{7,6},{8,9},{9,8},{10,11... | collective-permute-start | bytes 92168 | tf_op jit(solution)/shard_map/ppermute | solution.py:428
  189.6 11.1 %collective-permute-start.4 = (bf16[384,1152]{1,0:T(8,128)(2,1)S(1)}, bf16[384,1152]{1,0:T(8,128)(2,1)S(1)}, u32[]{:S(2)}, u32[]{:S(2)}) collective-permute-start(bf16[384,1152]{1,0:T(8,128)(2,1)S(1)} %dynamic-slice_bitcast_fusion), channel_id=1, source_target_pairs={{0,2},{1,3},{2,0},{3,1},{4,6},{5,7},{6,4},{7,5},{8,10},{9,11},{10,... | collective-permute-start | bytes 2654216 | tf_op jit(solution)/shard_map/ppermute | solution.py:428
  191.0 4.5 %collective-permute-start.16 = (f32[2,384]{1,0:T(2,128)S(1)}, f32[2,384]{1,0:T(2,128)S(1)}, u32[]{:S(2)}, u32[]{:S(2)}) collective-permute-start(f32[2,384]{1,0:T(2,128)S(1)} %add.247), channel_id=1, source_target_pairs={{0,8},{1,9},{2,10},{3,11},{4,12},{5,13},{6,14},{7,15},{8,0},{9,1},... | collective-permute-start | bytes 9224 | tf_op jit(solution)/shard_map/ppermute | solution.py:428
  193.1 5.0 %collective-permute-start.29 = (f32[10,768]{1,0:T(8,128)S(1)}, f32[10,768]{1,0:T(8,128)S(1)}, u32[]{:S(2)}, u32[]{:S(2)}) collective-permute-start(f32[10,768]{1,0:T(8,128)S(1)} %add.256), channel_id=1, source_target_pairs={{0,4},{1,5},{2,6},{3,7},{4,0},{5,1},{6,2},{7,3},{8,12},{9,13},{10,... | collective-permute-start | bytes 92168 | tf_op jit(solution)/shard_map/ppermute | solution.py:428
  194.3 5.6 %collective-permute-start.20 = (bf16[96,768]{1,0:T(8,128)(2,1)S(1)}, bf16[96,768]{1,0:T(8,128)(2,1)S(1)}, u32[]{:S(2)}, u32[]{:S(2)}) collective-permute-start(bf16[96,768]{1,0:T(8,128)(2,1)S(1)} %dynamic-slice_bitcast_fusion.12), channel_id=1, source_target_pairs={{0,4},{1,5},{2,6},{3,7},{4,0},{5,1},{6,2},{7,3},{8,12},{9,13},{10,... | collective-permute-start | bytes 442376 | tf_op jit(solution)/shard_map/ppermute | solution.py:428
  195.4 16.6 %collective-permute-start.3 = (bf16[384,1152]{1,0:T(8,128)(2,1)S(1)}, bf16[384,1152]{1,0:T(8,128)(2,1)S(1)}, u32[]{:S(2)}, u32[]{:S(2)}) collective-permute-start(bf16[384,1152]{1,0:T(8,128)(2,1)S(1)} %dynamic-slice_bitcast_fusion.1), channel_id=1, source_target_pairs={{0,2},{1,3},{2,0},{3,1},{4,6},{5,7},{6,4},{7,5},{8,10},{9,11},{10,... | collective-permute-start | bytes 2654216 | tf_op jit(solution)/shard_map/ppermute | solution.py:428
  195.5 15.1 %collective-permute-start.17 = (f32[2,384]{1,0:T(2,128)S(1)}, f32[2,384]{1,0:T(2,128)S(1)}, u32[]{:S(2)}, u32[]{:S(2)}) collective-permute-start(f32[2,384]{1,0:T(2,128)S(1)} %add.248), channel_id=1, source_target_pairs={{0,16},{1,17},{2,18},{3,19},{4,20},{5,21},{6,22},{7,23},{8,24},{9,... | collective-permute-start | bytes 9224 | tf_op jit(solution)/shard_map/ppermute | solution.py:428
  198.2 12.4 %collective-permute-start.30 = (f32[10,768]{1,0:T(8,128)S(1)}, f32[10,768]{1,0:T(8,128)S(1)}, u32[]{:S(2)}, u32[]{:S(2)}) collective-permute-start(f32[10,768]{1,0:T(8,128)S(1)} %add.257), channel_id=1, source_target_pairs={{0,8},{1,9},{2,10},{3,11},{4,12},{5,13},{6,14},{7,15},{8,0},{9,1},... | collective-permute-start | bytes 92168 | tf_op jit(solution)/shard_map/ppermute | solution.py:428
  199.9 4.4 %collective-permute-start.21 = (bf16[48,768]{1,0:T(8,128)(2,1)S(1)}, bf16[48,768]{1,0:T(8,128)(2,1)S(1)}, u32[]{:S(2)}, u32[]{:S(2)}) collective-permute-start(bf16[48,768]{1,0:T(8,128)(2,1)S(1)} %dynamic-slice_bitcast_fusion.14), channel_id=1, source_target_pairs={{0,8},{1,9},{2,10},{3,11},{4,12},{5,13},{6,14},{7,15},{8,0},{9,1},... | collective-permute-start | bytes 221192 | tf_op jit(solution)/shard_map/ppermute | solution.py:428
  200.8 20.9 %collective-permute-start.5 = (bf16[384,1152]{1,0:T(8,128)(2,1)S(1)}, bf16[384,1152]{1,0:T(8,128)(2,1)S(1)}, u32[]{:S(2)}, u32[]{:S(2)}) collective-permute-start(bf16[384,1152]{1,0:T(8,128)(2,1)S(1)} %bitcast_add_fusion.2), channel_id=1, source_target_pairs={{0,1},{1,0},{2,3},{3,2},{4,5},{5,4},{6,7},{7,6},{8,9},{9,8},{10,11... | collective-permute-start | bytes 2654216 | tf_op jit(solution)/shard_map/ppermute | solution.py:428
  204.3 6.8 %collective-permute-start.22 = (bf16[48,768]{1,0:T(8,128)(2,1)S(1)}, bf16[48,768]{1,0:T(8,128)(2,1)S(1)}, u32[]{:S(2)}, u32[]{:S(2)}) collective-permute-start(bf16[48,768]{1,0:T(8,128)(2,1)S(1)} %bitcast_add_fusion.15), channel_id=1, source_target_pairs={{0,16},{1,17},{2,18},{3,19},{4,20},{5,21},{6,22},{7,23},{8,24},{9,... | collective-permute-start | bytes 221192 | tf_op jit(solution)/shard_map/ppermute | solution.py:428
  210.6 47.6 %collective-permute-start.32 = (bf16[8,192,768]{2,1,0:T(8,128)(2,1)S(1)}, bf16[8,192,768]{2,1,0:T(8,128)(2,1)S(1)}, u32[]{:S(2)}, u32[]{:S(2)}) collective-permute-start(bf16[8,192,768]{2,1,0:T(8,128)(2,1)S(1)} %copy-done.36), channel_id=1, source_target_pairs={{0,2},{1,3},{2,0},{3,1},{4,6},{5,7},{6,4},{7,5},{8,10},{9,11},{10,... | collective-permute-start | bytes 7077896 | tf_op jit(solution)/shard_map/ppermute | solution.py:428
  210.6 54.5 %collective-permute-start.37 = (bf16[8,192,768]{2,1,0:T(8,128)(2,1)}, bf16[8,192,768]{2,1,0:T(8,128)(2,1)}, u32[]{:S(2)}, u32[]{:S(2)}) collective-permute-start(bf16[8,192,768]{2,1,0:T(8,128)(2,1)} %get-tuple-element.72), channel_id=1, source_target_pairs={{0,2},{1,3},{2,0},{3,1},{4,6},{5,7},{6,4},{7,5},{8,10},{9,11},{10,... | collective-permute-start | bytes 7077896 | tf_op jit(solution)/shard_map/ppermute | solution.py:428
  211.1 12.5 %collective-permute-start.31 = (f32[10,768]{1,0:T(8,128)S(1)}, f32[10,768]{1,0:T(8,128)S(1)}, u32[]{:S(2)}, u32[]{:S(2)}) collective-permute-start(f32[10,768]{1,0:T(8,128)S(1)} %add.258), channel_id=1, source_target_pairs={{0,16},{1,17},{2,18},{3,19},{4,20},{5,21},{6,22},{7,23},{8,24},{9,... | collective-permute-start | bytes 92168 | tf_op jit(solution)/shard_map/ppermute | solution.py:428
  212.0 11.6 %collective-permute-start.23 = (bf16[48,768]{1,0:T(8,128)(2,1)S(1)}, bf16[48,768]{1,0:T(8,128)(2,1)S(1)}, u32[]{:S(2)}, u32[]{:S(2)}) collective-permute-start(bf16[48,768]{1,0:T(8,128)(2,1)S(1)} %add.254), channel_id=1, source_target_pairs={{0,8},{1,9},{2,10},{3,11},{4,12},{5,13},{6,14},{7,15},{8,0},{9,1},... | collective-permute-start | bytes 221192 | tf_op jit(solution)/shard_map/ppermute | solution.py:428
  221.9 12.1 %collective-permute-start.6 = (bf16[192,1152]{1,0:T(8,128)(2,1)S(1)}, bf16[192,1152]{1,0:T(8,128)(2,1)S(1)}, u32[]{:S(2)}, u32[]{:S(2)}) collective-permute-start(bf16[192,1152]{1,0:T(8,128)(2,1)S(1)} %dynamic-slice_bitcast_fusion.5), channel_id=1, source_target_pairs={{0,4},{1,5},{2,6},{3,7},{4,0},{5,1},{6,2},{7,3},{8,12},{9,13},{10,... | collective-permute-start | bytes 1327112 | tf_op jit(solution)/shard_map/ppermute | solution.py:428
  223.7 12.4 %collective-permute-start.24 = (bf16[96,768]{1,0:T(8,128)(2,1)S(1)}, bf16[96,768]{1,0:T(8,128)(2,1)S(1)}, u32[]{:S(2)}, u32[]{:S(2)}) collective-permute-start(bf16[96,768]{1,0:T(8,128)(2,1)S(1)} %pad_maximum_fusion.9), channel_id=1, source_target_pairs={{0,4},{1,5},{2,6},{3,7},{4,0},{5,1},{6,2},{7,3},{8,12},{9,13},{10,... | collective-permute-start | bytes 442376 | tf_op jit(solution)/shard_map/ppermute | solution.py:428
  234.1 7.2 %collective-permute-start.7 = (bf16[96,1152]{1,0:T(8,128)(2,1)S(1)}, bf16[96,1152]{1,0:T(8,128)(2,1)S(1)}, u32[]{:S(2)}, u32[]{:S(2)}) collective-permute-start(bf16[96,1152]{1,0:T(8,128)(2,1)S(1)} %dynamic-slice_bitcast_fusion.9), channel_id=1, source_target_pairs={{0,8},{1,9},{2,10},{3,11},{4,12},{5,13},{6,14},{7,15},{8,0},{9,1},... | collective-permute-start | bytes 663560 | tf_op jit(solution)/shard_map/ppermute | solution.py:428
  241.4 9.3 %collective-permute-start.8 = (bf16[48,1152]{1,0:T(8,128)(2,1)S(1)}, bf16[48,1152]{1,0:T(8,128)(2,1)S(1)}, u32[]{:S(2)}, u32[]{:S(2)}) collective-permute-start(bf16[48,1152]{1,0:T(8,128)(2,1)S(1)} %dynamic-slice_bitcast_fusion.13), channel_id=1, source_target_pairs={{0,16},{1,17},{2,18},{3,19},{4,20},{5,21},{6,22},{7,23},{8,24},{9,... | collective-permute-start | bytes 331784 | tf_op jit(solution)/shard_map/ppermute | solution.py:428
  241.5 9.2 %collective-permute-start.25 = (bf16[192,768]{1,0:T(8,128)(2,1)S(1)}, bf16[192,768]{1,0:T(8,128)(2,1)S(1)}, u32[]{:S(2)}, u32[]{:S(2)}) collective-permute-start(bf16[192,768]{1,0:T(8,128)(2,1)S(1)} %pad_maximum_fusion.7), channel_id=1, source_target_pairs={{0,2},{1,3},{2,0},{3,1},{4,6},{5,7},{6,4},{7,5},{8,10},{9,11},{10,... | collective-permute-start | bytes 884744 | tf_op jit(solution)/shard_map/ppermute | solution.py:428
  250.6 6.0 %collective-permute-start.9 = (bf16[48,1152]{1,0:T(8,128)(2,1)S(1)}, bf16[48,1152]{1,0:T(8,128)(2,1)S(1)}, u32[]{:S(2)}, u32[]{:S(2)}) collective-permute-start(bf16[48,1152]{1,0:T(8,128)(2,1)S(1)} %bitcast_add_fusion.14), channel_id=1, source_target_pairs={{0,16},{1,17},{2,18},{3,19},{4,20},{5,21},{6,22},{7,23},{8,24},{9,... | collective-permute-start | bytes 331784 | tf_op jit(solution)/shard_map/ppermute | solution.py:428
  256.7 6.0 %collective-permute-start.10 = (bf16[96,1152]{1,0:T(8,128)(2,1)S(1)}, bf16[96,1152]{1,0:T(8,128)(2,1)S(1)}, u32[]{:S(2)}, u32[]{:S(2)}) collective-permute-start(bf16[96,1152]{1,0:T(8,128)(2,1)S(1)} %pad_maximum_fusion.8), channel_id=1, source_target_pairs={{0,8},{1,9},{2,10},{3,11},{4,12},{5,13},{6,14},{7,15},{8,0},{9,1},... | collective-permute-start | bytes 663560 | tf_op jit(solution)/shard_map/ppermute | solution.py:428
  257.6 12.8 %collective-permute-start.26 = (bf16[384,768]{1,0:T(8,128)(2,1)}, bf16[384,768]{1,0:T(8,128)(2,1)}, u32[]{:S(2)}, u32[]{:S(2)}) collective-permute-start(bf16[384,768]{1,0:T(8,128)(2,1)} %pad_maximum_fusion.5), channel_id=1, source_target_pairs={{0,1},{1,0},{2,3},{3,2},{4,5},{5,4},{6,7},{7,6},{8,9},{9,8},{10,11... | collective-permute-start | bytes 1769480 | tf_op jit(solution)/shard_map/ppermute | solution.py:428
  260.0 32.7 %collective-permute-start.33 = (bf16[2,2,2,96,768]{4,3,1,0,2:T(8,128)(2,1)}, bf16[2,2,2,96,768]{4,3,1,0,2:T(8,128)(2,1)S(1)}, u32[]{:S(2)}, u32[]{:S(2)}) collective-permute-start(bf16[2,2,2,96,768]{4,3,1,0,2:T(8,128)(2,1)} %bitcast.109), channel_id=1, source_target_pairs={{0,4},{1,5},{2,6},{3,7},{4,0},{5,1},{6,2},{7,3},{8,12},{9,13},{10,... | collective-permute-start | bytes 3538952 | tf_op jit(solution)/shard_map/ppermute | solution.py:428
  263.6 27.9 %collective-permute-start.11 = (bf16[192,1152]{1,0:T(8,128)(2,1)}, bf16[192,1152]{1,0:T(8,128)(2,1)}, u32[]{:S(2)}, u32[]{:S(2)}) collective-permute-start(bf16[192,1152]{1,0:T(8,128)(2,1)} %pad_maximum_fusion.6), channel_id=1, source_target_pairs={{0,4},{1,5},{2,6},{3,7},{4,0},{5,1},{6,2},{7,3},{8,12},{9,13},{10,... | collective-permute-start | bytes 1327112 | tf_op jit(solution)/shard_map/ppermute | solution.py:428
  268.3 29.0 %collective-permute-start.38 = (bf16[2,2,2,96,768]{4,3,1,0,2:T(8,128)(2,1)S(1)}, bf16[2,2,2,96,768]{4,3,1,0,2:T(8,128)(2,1)S(1)}, u32[]{:S(2)}, u32[]{:S(2)}) collective-permute-start(bf16[2,2,2,96,768]{4,3,1,0,2:T(8,128)(2,1)S(1)} %bitcast.126), channel_id=1, source_target_pairs={{0,1},{1,0},{2,3},{3,2},{4,5},{5,4},{6,7},{7,6},{8,9},{9,8},{10,11... | collective-permute-start | bytes 3538952 | tf_op jit(solution)/shard_map/ppermute | solution.py:428
  292.9 12.7 %collective-permute-start.34 = (bf16[2,2,96,768]{3,2,1,0:T(8,128)(2,1)S(1)}, bf16[2,2,96,768]{3,2,1,0:T(8,128)(2,1)S(1)}, u32[]{:S(2)}, u32[]{:S(2)}) collective-permute-start(bf16[2,2,96,768]{3,2,1,0:T(8,128)(2,1)S(1)} %dynamic-slice_bitcast_fusion.4), channel_id=1, source_target_pairs={{0,1},{1,0},{2,3},{3,2},{4,5},{5,4},{6,7},{7,6},{8,9},{9,8},{10,11... | collective-permute-start | bytes 1769480 | tf_op jit(solution)/shard_map/ppermute | solution.py:428
  297.5 10.3 %collective-permute-start.39 = (bf16[2,2,96,768]{3,2,1,0:T(8,128)(2,1)S(1)}, bf16[2,2,96,768]{3,2,1,0:T(8,128)(2,1)S(1)}, u32[]{:S(2)}, u32[]{:S(2)}) collective-permute-start(bf16[2,2,96,768]{3,2,1,0:T(8,128)(2,1)S(1)} %dynamic-slice_bitcast_fusion.3), channel_id=1, source_target_pairs={{0,4},{1,5},{2,6},{3,7},{4,0},{5,1},{6,2},{7,3},{8,12},{9,13},{10,... | collective-permute-start | bytes 1769480 | tf_op jit(solution)/shard_map/ppermute | solution.py:428
  298.0 11.6 %collective-permute-start.12 = (bf16[384,1152]{1,0:T(8,128)(2,1)S(1)}, bf16[384,1152]{1,0:T(8,128)(2,1)S(1)}, u32[]{:S(2)}, u32[]{:S(2)}) collective-permute-start(bf16[384,1152]{1,0:T(8,128)(2,1)S(1)} %pad_maximum_fusion.4), channel_id=1, source_target_pairs={{0,2},{1,3},{2,0},{3,1},{4,6},{5,7},{6,4},{7,5},{8,10},{9,11},{10,... | collective-permute-start | bytes 2654216 | tf_op jit(solution)/shard_map/ppermute | solution.py:428
  305.7 9.8 %collective-permute-start.35 = (bf16[2,96,768]{2,1,0:T(8,128)(2,1)S(1)}, bf16[2,96,768]{2,1,0:T(8,128)(2,1)S(1)}, u32[]{:S(2)}, u32[]{:S(2)}) collective-permute-start(bf16[2,96,768]{2,1,0:T(8,128)(2,1)S(1)} %dynamic-slice_bitcast_fusion.7), channel_id=1, source_target_pairs={{0,8},{1,9},{2,10},{3,11},{4,12},{5,13},{6,14},{7,15},{8,0},{9,1},... | collective-permute-start | bytes 884744 | tf_op jit(solution)/shard_map/ppermute | solution.py:428
  307.9 12.0 %collective-permute-start.40 = (bf16[2,96,768]{2,1,0:T(8,128)(2,1)S(1)}, bf16[2,96,768]{2,1,0:T(8,128)(2,1)S(1)}, u32[]{:S(2)}, u32[]{:S(2)}) collective-permute-start(bf16[2,96,768]{2,1,0:T(8,128)(2,1)S(1)} %dynamic-slice_bitcast_fusion.6), channel_id=1, source_target_pairs={{0,8},{1,9},{2,10},{3,11},{4,12},{5,13},{6,14},{7,15},{8,0},{9,1},... | collective-permute-start | bytes 884744 | tf_op jit(solution)/shard_map/ppermute | solution.py:428
  315.6 7.9 %collective-permute-start.36 = (bf16[96,768]{1,0:T(8,128)(2,1)S(1)}, bf16[96,768]{1,0:T(8,128)(2,1)S(1)}, u32[]{:S(2)}, u32[]{:S(2)}) collective-permute-start(bf16[96,768]{1,0:T(8,128)(2,1)S(1)} %dynamic-slice_bitcast_fusion.11), channel_id=1, source_target_pairs={{0,16},{1,17},{2,18},{3,19},{4,20},{5,21},{6,22},{7,23},{8,24},{9,... | collective-permute-start | bytes 442376 | tf_op jit(solution)/shard_map/ppermute | solution.py:428
  320.0 6.1 %collective-permute-start.41 = (bf16[96,768]{1,0:T(8,128)(2,1)S(1)}, bf16[96,768]{1,0:T(8,128)(2,1)S(1)}, u32[]{:S(2)}, u32[]{:S(2)}) collective-permute-start(bf16[96,768]{1,0:T(8,128)(2,1)S(1)} %dynamic-slice_bitcast_fusion.10), channel_id=1, source_target_pairs={{0,16},{1,17},{2,18},{3,19},{4,20},{5,21},{6,22},{7,23},{8,24},{9,... | collective-permute-start | bytes 442376 | tf_op jit(solution)/shard_map/ppermute | solution.py:428
  (36 other events, 240.8 us)

commit v2 on v1

v2 whole, which is shorter than its diff:
```python
import functools

import jax
import jax.numpy as jnp
from jax import lax
from jax.experimental import pallas as pl
from jax.experimental.pallas import tpu as pltpu
from jax.sharding import PartitionSpec as P

HEAD_DIM = 64
MICRO = 4
F32 = jnp.float32
BF16 = jnp.bfloat16
NORM_EPS = 1e-05
MASK = 2.0**30
AXES = ("dp", "head")


def dims(left, right, left_dim, right_dim):
    return lax.dot_general(
        left, right, (((left_dim,), (right_dim,)), ((), ())), preferred_element_type=F32
    )


def matmul(left, right):
    return jnp.dot(left, right, preferred_element_type=F32)


def query_marks(labels, shape):
    lane = lax.broadcasted_iota(jnp.int32, shape, 1)
    return jnp.where((lane & 63) == labels, 1.0, 0.0).astype(BF16)


def key_marks(labels, shape):
    lane = lax.broadcasted_iota(jnp.int32, shape, 1) & 63
    return jnp.where((lane < 4) & (lane != labels), -MASK, 0.0).astype(BF16)


def attend_forward(q_ref, k_ref, v_ref, lab_ref, out_ref, log_ref):
    labels = lab_ref[0]
    shape = (labels.shape[0], 128)
    low = lax.broadcasted_iota(jnp.int32, shape, 1) < HEAD_DIM
    q_extra, k_extra = query_marks(labels, shape), key_marks(labels, shape)
    q = q_ref[...] * jnp.asarray(0.125, BF16)
    k, v = k_ref[...], v_ref[...]
    outs = []
    for t in range(2):
        mine = low if t == 0 else jnp.logical_not(low)
        scores = dims(jnp.where(mine, k, k_extra), jnp.where(mine, q, q_extra), 1, 1)
        largest = jnp.max(scores, axis=0, keepdims=True)
        soft = jnp.exp(scores - largest)
        total = jnp.sum(soft, axis=0, keepdims=True)
        out = dims(v, soft.astype(BF16), 0, 0)
        outs.append(out[t * HEAD_DIM : (t + 1) * HEAD_DIM] * (1.0 / total))
        log_ref[0, 0, t : t + 1] = largest + jnp.log(total)
    out_ref[...] = jnp.concatenate(outs, axis=0).T.astype(BF16)


def run_attend_forward(qkv, labels, seq):
    rows = qkv.shape[0]
    pairs = qkv.shape[1] // (3 * 128)
    part = lambda which: pl.BlockSpec((seq, 128), lambda s, p: (s, which * pairs + p))
    return pl.pallas_call(
        attend_forward,
        grid=(rows // seq, pairs),
        in_specs=[part(0), part(1), part(2), pl.BlockSpec((1, seq, 1), lambda s, p: (s, 0, 0))],
        out_specs=[part(0), pl.BlockSpec((1, 1, 2, seq), lambda s, p: (s, p, 0, 0))],
        out_shape=[
            jax.ShapeDtypeStruct((rows, pairs * 128), BF16),
            jax.ShapeDtypeStruct((rows // seq, pairs, 2, seq), F32),
        ],
        compiler_params=pltpu.CompilerParams(vmem_limit_bytes=40 << 20),
        cost_estimate=pl.CostEstimate(
            flops=rows * pairs * 2 * seq * 256 * 2 * 2, bytes_accessed=4 << 20, transcendentals=0
        ),
        name="attend_forward",
    )(qkv, qkv, qkv, labels)


def attend_backward(
    core_ref,
    q_ref,
    k_ref,
    v_ref,
    out_ref,
    grad_ref,
    lab_ref,
    log_ref,
    x_keep,
    x_send,
    grads_ref,
    keep_ref,
    send_ref,
    keep_sum,
    send_sum,
    bias_sum,
):
    step, pair = pl.program_id(0), pl.program_id(1)
    labels = lab_ref[0]
    shape = (labels.shape[0], 128)
    low = lax.broadcasted_iota(jnp.int32, shape, 1) < HEAD_DIM
    q_extra, k_extra = query_marks(labels, shape), key_marks(labels, shape)
    q = q_ref[...] * jnp.asarray(0.125, BF16)
    k, v, grad = k_ref[...], v_ref[...], grad_ref[...]
    zero = jnp.zeros_like(q)
    inner = (grad.astype(F32) * out_ref[...].astype(F32)).T
    dqs, dks, dvs = [], [], []
    for t in range(2):
        mine = low if t == 0 else jnp.logical_not(low)
        half = slice(t * HEAD_DIM, (t + 1) * HEAD_DIM)
        scores = dims(jnp.where(mine, k, k_extra), jnp.where(mine, q, q_extra), 1, 1)
        soft = jnp.exp(scores - log_ref[0, 0, t : t + 1])
        grad_soft = dims(v, jnp.where(mine, grad, zero), 1, 1)
        row_inner = jnp.sum(inner[half], axis=0, keepdims=True)
        grad_scores = (soft * (grad_soft - row_inner)).astype(BF16)
        dvs.append(dims(soft.astype(BF16), grad, 1, 0))
        dks.append(dims(grad_scores, q, 1, 0))
        dqs.append(dims(k, grad_scores, 0, 0)[half])
    n_pairs = pl.num_programs(1)
    found = (
        (jnp.concatenate(dqs, axis=0).T * 0.125).astype(BF16),
        jnp.where(low, dks[0], dks[1]).astype(BF16),
        jnp.where(low, dvs[0], dvs[1]).astype(BF16),
    )
    for i, value in enumerate(found):
        place = pl.multiple_of((i * n_pairs + pair) * 128, 128)
        grads_ref[:, pl.ds(place, 128)] = value

    @pl.when(pair == n_pairs - 1)
    def _():
        grads = grads_ref[...]
        keep, send = dims(x_keep[...], grads, 0, 0), dims(x_send[...], grads, 0, 0)
        bias = jnp.sum(grads.astype(F32), axis=0, keepdims=True)

        @pl.when(step == 0)
        def _():
            keep_sum[...] = keep
            send_sum[...] = send
            bias_sum[...] = bias

        @pl.when(step > 0)
        def _():
            keep_sum[...] += keep
            send_sum[...] += send
            bias_sum[...] += bias

        @pl.when(step == pl.num_programs(0) - 1)
        def _():
            cols = grads.shape[1]
            total = bias_sum[...]
            third = cols // 3
            parts = [total[:, i * 128 : (i + 1) * 128] for i in range(cols // 128)]
            parts = parts[: third // 128] + parts[2 * third // 128 :]
            rows = jnp.concatenate(parts, axis=0)
            rows = jnp.concatenate(
                [rows, jnp.zeros((keep_ref.shape[0] - rows.shape[0], 128), F32)], axis=0
            ).astype(BF16)
            for ref, value in ((keep_ref, keep_sum), (send_ref, send_sum)):
                ref[:, :cols] = value[...].astype(BF16)
                ref[:, cols:] = rows


def run_attend_backward(core, qkv, out, grad, labels, logsum, tokens, seq):
    rows, cols = qkv.shape
    pairs = cols // (3 * 128)
    half = tokens.shape[1] // 2
    part = lambda which: pl.BlockSpec((seq, 128), lambda s, p, c: (s, which * pairs + p))
    weight = jax.ShapeDtypeStruct((half, cols + 128), BF16)
    whole = pl.BlockSpec((half, cols + 128), lambda s, p, c: (0, 0))
    return pl.pallas_call(
        attend_backward,
        grid_spec=pltpu.PrefetchScalarGridSpec(
            num_scalar_prefetch=1,
            grid=(rows // seq, pairs),
            in_specs=[
                part(0),
                part(1),
                part(2),
                part(0),
                part(0),
                pl.BlockSpec((1, seq, 1), lambda s, p, c: (s, 0, 0)),
                pl.BlockSpec((1, 1, 2, seq), lambda s, p, c: (s, p, 0, 0)),
                pl.BlockSpec((seq, half), lambda s, p, c: (s, c[0])),
                pl.BlockSpec((seq, half), lambda s, p, c: (s, 1 - c[0])),
            ],
            out_specs=[pl.BlockSpec((seq, cols), lambda s, p, c: (s, 0)), whole, whole],
            scratch_shapes=[
                pltpu.VMEM((half, cols), F32),
                pltpu.VMEM((half, cols), F32),
                pltpu.VMEM((1, cols), F32),
            ],
        ),
        out_shape=[jax.ShapeDtypeStruct((rows, cols), BF16), weight, weight],
        compiler_params=pltpu.CompilerParams(vmem_limit_bytes=40 << 20),
        cost_estimate=pl.CostEstimate(
            flops=rows * pairs * 2 * seq * 256 * 2 * 3, bytes_accessed=8 << 20, transcendentals=0
        ),
        name="attend_backward",
    )(core, qkv, qkv, qkv, out, grad, labels, logsum, tokens, tokens)


def gelu_pair(inner):
    phi = 0.5 + 0.5 * lax.erf(inner * 0.7071067811865476)
    bell = jnp.exp(-0.5 * (inner * inner))
    return inner * phi, phi + inner * (bell * 0.3989422804014327)


def norm_parts(values):
    centered = values - jnp.mean(values, axis=-1, keepdims=True)
    factor = lax.rsqrt(jnp.mean(centered * centered, axis=-1, keepdims=True) + NORM_EPS)
    return centered * factor, factor


def norm_back(grad_out, normed, factor, gain):
    scaled = grad_out * gain
    return factor * (
        scaled
        - jnp.mean(scaled, axis=-1, keepdims=True)
        - normed * jnp.mean(scaled * normed, axis=-1, keepdims=True)
    )


def held(shape):
    return pl.BlockSpec(shape, lambda i, *_: (0,) * len(shape), pipeline_mode=pl.Buffered(1))


def add_sums(ref, *values):
    @pl.when(pl.program_id(0) == 0)
    def _():
        ref[...] = jnp.zeros_like(ref)

    for i, value in enumerate(values):
        ref[i : i + 1] += jnp.sum(value, axis=0, keepdims=True)


def feed_forward(
    seq,
    chunk,
    count,
    ctx_a,
    ctx_b,
    tokens,
    w_out,
    w_up,
    w_down,
    vectors,
    b_up,
    cotangent,
    y_ref,
    hidden_ref,
    normed_ref,
    factor_ref,
    act_ref,
    slope_ref,
    mid_ref,
    mid_low_ref,
    sums_ref,
):
    b_out, gain_one, shift_one, b_down, gain_two, shift_two = [
        vectors[i : i + 1] for i in range(6)
    ]
    context = jnp.concatenate([ctx_a[...], ctx_b[...]], axis=1)
    normed_one, factor_one = norm_parts(
        tokens[...].astype(F32) + matmul(context, w_out[...]) + b_out
    )
    normed_ref[...] = normed_one
    factor_ref[...] = jnp.broadcast_to(factor_one, factor_ref.shape)
    hidden = normed_one * gain_one + shift_one
    hidden_low = hidden.astype(BF16)
    hidden_ref[...] = hidden_low
    total = hidden + b_down
    for j in range(w_up.shape[1] // chunk):
        cols = slice(j * chunk, (j + 1) * chunk)
        activated, slope = gelu_pair(matmul(hidden_low, w_up[:, cols]) + b_up[:, cols])
        activated = activated.astype(BF16)
        act_ref[:, cols] = activated
        slope_ref[:, cols] = slope.astype(BF16)
        total = total + matmul(activated, w_down[cols, :])
    normed_two, factor_two = norm_parts(total)
    y_ref[...] = (normed_two * gain_two + shift_two).astype(BF16)
    block = tokens.shape[0]
    place = pl.program_id(0) * block + lax.broadcasted_iota(jnp.int32, (block, 1), 0)
    live = (place % seq // (seq // MICRO) < count[0]).astype(F32)
    grad_y = cotangent[...].astype(F32) * live
    grad_mid = norm_back(grad_y, normed_two, factor_two, gain_two)
    mid_ref[...] = grad_mid
    mid_low_ref[...] = grad_mid.astype(BF16)
    add_sums(sums_ref, grad_y * normed_two, grad_y, grad_mid)


def run_feed_forward(
    seq, count, ctx_a, ctx_b, tokens, w_out, w_up, w_down, vectors, b_up, cotangent, block=256
):
    rows, width = tokens.shape
    ff = w_up.shape[1]
    half = ctx_a.shape[1]
    token = lambda cols: pl.BlockSpec((block, cols), lambda i, c: (i, 0))
    out, near = jax.ShapeDtypeStruct, pltpu.VMEM
    return pl.pallas_call(
        functools.partial(feed_forward, seq, 1024),
        grid_spec=pltpu.PrefetchScalarGridSpec(
            num_scalar_prefetch=1,
            grid=(rows // block,),
            in_specs=[
                token(half),
                token(half),
                token(width),
                held(w_out.shape),
                held(w_up.shape),
                held(w_down.shape),
                held(vectors.shape),
                held(b_up.shape),
                token(width),
            ],
            out_specs=[token(c) for c in (width, width, width, 128, ff, ff, width, width)]
            + [pl.BlockSpec((8, width), lambda i, c: (0, 0))],
        ),
        out_shape=[
            out((rows, width), BF16),
            near((rows, width), BF16),
            out((rows, width), F32),
            out((rows, 128), F32),
            near((rows, ff), BF16),
            near((rows, ff), BF16),
            out((rows, width), F32),
            near((rows, width), BF16),
            out((8, width), F32),
        ],
        compiler_params=pltpu.CompilerParams(vmem_limit_bytes=34 << 20),
        cost_estimate=pl.CostEstimate(
            flops=4 * rows * width * (width + 2 * ff), bytes_accessed=30 << 20, transcendentals=0
        ),
        name="feed_forward",
    )(count, ctx_a, ctx_b, tokens, w_out, w_up, w_down, vectors, b_up, cotangent)


def weight_pieces(groups, group_rows, core_ref, left, right, keep, send):
    core = core_ref[0]
    result = dims(left[...], right[...], 0, 0)
    result = result.reshape(groups, 2, group_rows, result.shape[-1])
    keep[...] = jnp.where(core == 0, result[:, 0], result[:, 1]).astype(BF16)
    send[...] = jnp.where(core == 0, result[:, 1], result[:, 0]).astype(BF16)


def run_weight_pieces(core, left, right, rows_dev, block=768):
    rows, ff = left.shape
    width = right.shape[1]
    group_rows = 2 * rows_dev
    groups = block // (2 * group_rows)
    piece = pl.BlockSpec((groups, group_rows, width), lambda i, c: (i, 0, 0))
    shape = jax.ShapeDtypeStruct((ff // (2 * group_rows), group_rows, width), BF16)
    return pl.pallas_call(
        functools.partial(weight_pieces, groups, group_rows),
        grid_spec=pltpu.PrefetchScalarGridSpec(
            num_scalar_prefetch=1,
            grid=(ff // block,),
            in_specs=[pl.BlockSpec((rows, block), lambda i, c: (0, i)), held((rows, width))],
            out_specs=[piece, piece],
        ),
        out_shape=[shape, shape],
        compiler_params=pltpu.CompilerParams(vmem_limit_bytes=24 << 20),
        cost_estimate=pl.CostEstimate(
            flops=4 * rows * width * ff, bytes_accessed=12 << 20, transcendentals=0
        ),
        name="weight_pieces",
    )(core, left, right)


def inner_gradient(mid_low, w_down, slope, *refs):
    out, sums = refs[-2:]
    grad = (dims(mid_low[...], w_down[...], 1, 1) * slope[...].astype(F32)).astype(BF16)
    out[...] = grad
    sums[...] = jnp.sum(grad.astype(F32), axis=0, keepdims=True)


def run_inner_gradient(mid_low, w_down, slope, part, parts, before=None, block=768):
    rows, width = mid_low.shape
    ff = w_down.shape[0]
    steps = ff // parts // block
    columns = pl.BlockSpec((rows, block), lambda i: (0, part * steps + i))
    args = [mid_low, w_down, slope] + ([] if before is None else [before])
    return pl.pallas_call(
        inner_gradient,
        grid=(steps,),
        in_specs=[
            held((rows, width)),
            pl.BlockSpec((block, width), lambda i: (part * steps + i, 0)),
            columns,
        ]
        + [pl.BlockSpec(memory_space=pl.ANY)] * (len(args) - 3),
        out_specs=[columns, pl.BlockSpec((1, block), lambda i: (0, i))],
        out_shape=[
            pltpu.VMEM((rows, ff), BF16),
            jax.ShapeDtypeStruct((1, ff // parts), F32),
        ],
        input_output_aliases={3: 0} if before is not None else {},
        compiler_params=pltpu.CompilerParams(vmem_limit_bytes=24 << 20),
        cost_estimate=pl.CostEstimate(
            flops=4 * rows * width * ff // parts, bytes_accessed=16 << 20, transcendentals=0
        ),
        name="inner_gradient",
    )(*args)


def first_gradient(
    grad_inner,
    mid,
    w_up,
    w_out,
    ctx_a,
    ctx_b,
    normed,
    factor,
    gain_one,
    first_ref,
    grad_ctx_a,
    grad_ctx_b,
    w_out_ref,
    sums_ref,
    total,
):
    step = pl.program_id(0)
    grad = mid[...] + dims(grad_inner[...], w_up[...], 1, 1)
    normed_one = normed[...]
    grad_first = norm_back(grad, normed_one, factor[:, :1], gain_one[...])
    first_ref[...] = grad_first
    add_sums(sums_ref, grad * normed_one, grad, grad_first)
    first_low = grad_first.astype(BF16)
    grad_ctx = dims(first_low, w_out[...], 1, 1).astype(BF16)
    half = grad_ctx_a.shape[1]
    grad_ctx_a[...] = grad_ctx[:, :half]
    grad_ctx_b[...] = grad_ctx[:, half:]

    @pl.when(step == 0)
    def _():
        total[...] = jnp.zeros_like(total)

    context = jnp.concatenate([ctx_a[...], ctx_b[...]], axis=1)
    total[...] += dims(context, first_low, 0, 0)

    @pl.when(step == pl.num_programs(0) - 1)
    def _():
        w_out_ref[...] = total[...].astype(BF16)


def run_first_gradient(
    grad_inner, mid, w_up, w_out, ctx_a, ctx_b, normed, factor, gain_one, block=256
):
    rows, width = mid.shape
    ff = w_up.shape[1]
    half = ctx_a.shape[1]
    token = lambda cols: pl.BlockSpec((block, cols), lambda i: (i, 0))
    out = jax.ShapeDtypeStruct
    return pl.pallas_call(
        first_gradient,
        grid=(rows // block,),
        in_specs=[
            token(ff),
            token(width),
            held(w_up.shape),
            held(w_out.shape),
            token(half),
            token(half),
            token(width),
            token(128),
            held((1, width)),
        ],
        out_specs=[token(width), token(half), token(half), held((width, width)), held((8, width))],
        out_shape=[
            out((rows, width), F32),
            out((rows, half), BF16),
            out((rows, half), BF16),
            out((width, width), BF16),
            out((8, width), F32),
        ],
        scratch_shapes=[pltpu.VMEM((width, width), F32)],
        compiler_params=pltpu.CompilerParams(vmem_limit_bytes=32 << 20),
        cost_estimate=pl.CostEstimate(
            flops=4 * rows * width * (ff + 2 * width), bytes_accessed=24 << 20, transcendentals=0
        ),
        name="first_gradient",
    )(grad_inner, mid, w_up, w_out, ctx_a, ctx_b, normed, factor, gain_one)


class Cube:
    def __init__(self, mesh):
        self.size = mesh.shape["dp"] * mesh.shape["head"]
        self.n_bits = self.size.bit_length() - 1
        self.upper = list(range(2, self.n_bits))
        self.index = lax.axis_index("dp") * mesh.shape["head"] + lax.axis_index("head")

    def bit(self, which):
        return (self.index >> which) & 1

    def swap(self, value, which):
        pairs = [(i, i ^ (1 << which)) for i in range(self.size)]
        return lax.ppermute(value, AXES, pairs)

    def half(self, value, axis, which, mine):
        bit = self.bit(which) if mine else 1 - self.bit(which)
        return lax.dynamic_index_in_dim(value, bit, axis, keepdims=False)

    def join(self, value, other, which):
        first = self.bit(which) == 0
        return jnp.concatenate(
            [jnp.where(first, value, other), jnp.where(first, other, value)], axis=0
        )


    def scatter_pieces(self, keep, send, rows_dev):
        (other,) = yield [(send, 1)]
        value = keep + other
        bits = list(range(self.n_bits - 1, 1, -1)) + [0]
        value = value.reshape((2,) * len(bits) + (rows_dev, value.shape[-1]))
        middle = value.shape[-1] // 2
        values = [value[..., :middle], value[..., middle:]]
        orders = [[0, 2], [2, 0]]
        left = [list(bits), list(bits)]
        while orders[0]:
            steps = [order.pop(0) for order in orders]
            axes = [held_bits.index(step) for held_bits, step in zip(left, steps)]
            others = yield [
                (self.half(value, axis, step, False), step)
                for value, axis, step in zip(values, axes, steps)
            ]
            values = [
                self.half(value, axis, step, True) + other
                for value, axis, step, other in zip(values, axes, steps, others)
            ]
            for held_bits, step in zip(left, steps):
                held_bits.remove(step)
        value, bits = jnp.concatenate(values, axis=-1), left[0]
        for step in self.upper[1:]:
            axis = bits.index(step)
            (other,) = yield [(self.half(value, axis, step, False), step)]
            value = self.half(value, axis, step, True) + other
            bits.remove(step)
        return value

    def reduce_rows(self, value, order):
        halved = []
        for which in order:
            rows = value.shape[0]
            if rows % 32 == 0:
                value = value.reshape(2, rows // 2, value.shape[1])
                (other,) = yield [(self.half(value, 0, which, False), which)]
                value = self.half(value, 0, which, True) + other
                halved.append(which)
            else:
                value = lax.optimization_barrier(value)
                (other,) = yield [(value, which)]
                value = value + other
        return value, halved

    def gather_rows(self, value, halved):
        for which in reversed(halved):
            (other,) = yield [(value, which)]
            value = self.join(value, other, which)
        return value

    def sum_out(self, own, peer):
        rows, width = own.shape
        value = jnp.concatenate([own, peer], axis=1).reshape(2, rows // 2, 2 * width)
        (other,) = yield [(self.half(value, 0, 1, False), 1)]
        value = self.half(value, 0, 1, True) + other
        value, halved = yield from self.reduce_rows(value, self.upper)
        (other,) = yield [(value[:, width:], 0)]
        value = value[:, :width] + other
        (other,) = yield [(value, 0)]
        value = jnp.concatenate([value, other], axis=1)
        value = yield from self.gather_rows(value, [1] + halved)
        return value[:, :width], value[:, width:]

    def peer_piece(self, keep, send, middle):
        (other,) = yield [(send, 1)]
        value = keep + other
        rows = value.shape[0] // 2
        right = value[:, middle:].reshape(2, rows, -1)
        left, other = yield [(value[:, :middle], 0), (self.half(right, 0, 2, False), 2)]
        right = self.half(right, 0, 2, True) + other
        (right,) = yield [(right, 0)]
        return left, right

    def own_piece(self, keep, send, middle, peer):
        (other,) = yield [(send, 1)]
        value = keep + other
        value = jnp.concatenate([value[:, :middle] + peer.result[0], value[:, middle:]], axis=1)
        value = value.reshape(2, value.shape[0] // 2, value.shape[1])
        (other,) = yield [(self.half(value, 0, 2, False), 2)]
        value = self.half(value, 0, 2, True) + other
        value = jnp.concatenate([value[:, :middle], value[:, middle:] + peer.result[1]], axis=1)
        value, halved = yield from self.reduce_rows(value, self.upper[1:])
        return (yield from self.gather_rows(value, [1, 2] + halved))


class Stream:
    def __init__(self, cube, steps):
        self.cube, self.steps, self.result = cube, steps, None
        self.wants = None
        self.advance(None)

    def advance(self, got):
        try:
            self.wants = self.steps.send(got)
        except StopIteration as stop:
            self.wants, self.result = None, stop.value

    def swaps(self):
        return tuple(self.cube.swap(value, which) for value, which in self.wants)


def tick(streams, work, *carry):
    streams = [stream for stream in streams if stream.wants is not None]
    moved = tuple(stream.swaps() for stream in streams)
    moved, work, carry = lax.optimization_barrier((moved, work, carry))
    for stream, got in zip(streams, moved):
        stream.advance(list(got))
    return (work, *carry)


def shards(
    mesh,
    tokens,
    labels,
    micro_counts,
    w_query,
    b_query,
    w_key,
    w_value,
    b_value,
    w_out,
    b_out,
    gain_one,
    shift_one,
    w_up,
    b_up,
    w_down,
    b_down,
    gain_two,
    shift_two,
    cotangent,
):
    cube = Cube(mesh)
    rows, width = tokens.shape
    seq = labels.shape[1]
    half = w_query.shape[1]
    ff = w_up.shape[1]
    head, core = cube.bit(0), cube.bit(1)

    own_w = jnp.concatenate([w_query, w_key, w_value], axis=1)
    part = lax.dynamic_index_in_dim(own_w.reshape(2, width // 2, 3 * half), core, 0, False)
    own_rows = lax.dynamic_slice_in_dim(w_out, head * half, half, 0)
    peer_rows = lax.dynamic_slice_in_dim(w_out, (1 - head) * half, half, 0)
    w_out_turned = jnp.concatenate([own_rows, peer_rows], axis=0)
    n_seq = rows // seq
    marks = lax.dynamic_slice_in_dim(labels, head * n_seq, n_seq, 0)[:, :, None]
    vectors = jnp.stack(
        [b_out, gain_one, shift_one, b_down, gain_two, shift_two, b_down, b_down]
    )

    def project(weight, offset):
        return (matmul(tokens, weight) + offset.astype(F32)).astype(BF16)

    own_b = jnp.concatenate([b_query, jnp.zeros_like(b_query), b_value])
    own_qkv = project(own_w, own_b)
    own_ctx, own_log = run_attend_forward(own_qkv, marks, seq)
    arrived, peer_b, own_ctx = lax.optimization_barrier(
        (cube.swap(part, 0), cube.swap(own_b, 0), own_ctx)
    )
    peer_w = cube.join(arrived, cube.swap(arrived, 1), 1)
    peer_qkv = project(peer_w, peer_b)
    peer_ctx, peer_log = run_attend_forward(peer_qkv, marks, seq)

    (
        layer_output,
        hidden_low,
        normed_one,
        factor_one,
        activated,
        slope,
        grad_mid,
        mid_low,
        sums_two,
    ) = run_feed_forward(
        seq,
        micro_counts,
        own_ctx,
        peer_ctx,
        tokens,
        w_out_turned,
        w_up,
        w_down,
        vectors,
        b_up[None],
        cotangent,
    )
    rows_dev = ff // cube.size
    cores = core[None]
    stream = lambda steps: Stream(cube, steps)

    keep, send = run_weight_pieces(cores, activated, mid_low, rows_dev)
    (keep, send), mid_low = tick([], (keep, send), mid_low)
    down = stream(cube.scatter_pieces(keep, send, rows_dev))
    inner_one = run_inner_gradient(mid_low, w_down, slope, 0, 2)
    (grad_inner, b_up_one), mid_low = tick([down], tuple(inner_one), mid_low)
    grad_inner, b_up_two = run_inner_gradient(mid_low, w_down, slope, 1, 2, grad_inner)
    keep, send = run_weight_pieces(cores, grad_inner, hidden_low, rows_dev)
    (keep, send), grad_inner, b_up_two = tick([down], (keep, send), grad_inner, b_up_two)
    up = stream(cube.scatter_pieces(keep, send, rows_dev))
    first = run_first_gradient(
        grad_inner,
        grad_mid,
        w_up,
        w_out_turned,
        own_ctx,
        peer_ctx,
        normed_one,
        factor_one,
        gain_one[None],
    )
    (first,) = tick([down, up], tuple(first))
    grad_first, own_grad_ctx, peer_grad_ctx, out_local, sums_one = first

    small = [sums_one[:3], sums_two[:3], b_up_one.reshape(-1, width), b_up_two.reshape(-1, width)]
    small = jnp.concatenate(small, axis=0).astype(BF16)
    n_small = small.shape[0]
    small = small.reshape(2, -1, 128)
    side = small.shape[1]
    small = jnp.pad(small, ((0, 0), (0, half - side), (0, 0)))
    out = stream(
        cube.sum_out(
            jnp.concatenate([out_local[:half], cube.half(small, 0, 0, True)], axis=1),
            jnp.concatenate([out_local[half:], cube.half(small, 0, 0, False)], axis=1),
        )
    )

    def backward(qkv, ctx, grad_ctx, logsum):
        return tuple(
            run_attend_backward(cores, qkv, ctx, grad_ctx, marks, logsum, tokens, seq)
        )

    middle = (3 * half + 128) // 256 * 128
    found = backward(peer_qkv, peer_ctx, peer_grad_ctx, peer_log)
    (peer_grads, keep, send), own_grad_ctx = tick([up, down, out], found, own_grad_ctx)
    peer = stream(cube.peer_piece(keep, send, middle))
    grad_tokens = grad_first + dims(peer_grads, peer_w, 1, 1)
    grad_tokens, own_grad_ctx = tick([peer], grad_tokens, own_grad_ctx)
    found = backward(own_qkv, own_ctx, own_grad_ctx, own_log)
    (own_grads, keep, send), grad_tokens = tick([peer, up, out, down], found, grad_tokens)
    own = stream(cube.own_piece(keep, send, middle, peer))
    grad_tokens = grad_tokens + dims(own_grads, own_w, 1, 1)
    (grad_tokens,) = tick([peer, own, up, out], grad_tokens)
    streams = [own, up, out, down]
    while any(stream.wants is not None for stream in streams):
        tick(streams, ())

    weights = own.result
    grad_w_query, grad_w_key, grad_w_value = [
        weights[:, i * half : (i + 1) * half].astype(F32) for i in range(3)
    ]
    bias = weights[: 2 * half // 128, 3 * half :].astype(F32).reshape(2, half)
    mine, other = out.result
    first = head == 0
    both = jnp.concatenate(
        [jnp.where(first, mine, other), jnp.where(first, other, mine)], axis=0
    ).astype(F32)
    small = jnp.concatenate([both[:side, width:], both[half : half + side, width:]], axis=0)
    small = small.reshape(n_small, width)
    return (
        layer_output,
        grad_tokens,
        grad_w_query,
        bias[0],
        grad_w_key,
        grad_w_value,
        bias[1],
        both[:, :width],
        small[2],
        small[0],
        small[1],
        up.result.astype(F32).T,
        small[6:].reshape(ff),
        down.result.astype(F32),
        small[5],
        small[3],
        small[4],
    )


def solution(mesh):
    rows = P(("dp", "head"), None)
    placed = (rows, P("dp", None), P("dp"), P(None, "head"), P("head"), P(None, "head"))
    placed += (P(None, "head"), P("head")) + (P(),) * 10 + (rows,)
    columns = P(None, "head")
    out_specs = (rows, rows, columns, P("head"), columns, columns, P("head"))
    out_specs += (P(),) * 4 + (P(None, ("dp", "head")), P(), rows, P(), P(), P())
    return jax.shard_map(
        functools.partial(shards, mesh),
        mesh=mesh,
        in_specs=placed,
        out_specs=out_specs,
        check_vma=False,
    )
```

time: 330 us -> 284 us (0.86)
  waiting for transfers between devices: 116 us -> 63.1 us
  local copies, waits for them, and re-layouts: 22 us -> 34.4 us
  matrix products: 20.2 us -> 10.6 us
  other arithmetic: 17.6 us -> 24 us
    ppermute x42 -> x38, waiting for transfers between devices: 116 us -> 63.1 us  [swap(): return lax.ppermute(value, AXES, pairs)]
    unnamed x90 -> x128, local copies, waits for them, and re-layouts: 11.4 us -> 22.6 us
    dot_general x4 -> x2, matrix products: 13.7 us -> 4.45 us  [dims(): lax.dot_general(left, right, (((left_dim,), (right_dim,)), ((), ())), pre...]
    add x28 -> x25, other arithmetic: 4.49 us -> 12.2 us  [the longest x2 5.46 us: scatter_pieces(): value = keep + other]
    ppermute x42 -> x38, starting transfers between devices: 36.6 us -> 34.5 us  [swap(): return lax.ppermute(value, AXES, pairs)]
    pallas_call x4 -> x8, Pallas kernels: 93.7 us -> 92.1 us  [the longest x2 29.5 us: run_attend_backward(): pl.pallas_call(attend_backward, grid_spec=pltpu.PrefetchScalarGridSpec(nu...]
  transfers between devices with their start and end apart: 42 -> 38, of which waited for: 19 -> 15; matrix products, arithmetic and copies ran while one was open for 11% -> 11% of each run, Pallas kernels for 3% -> 25%
where the time goes in v2:
time: 284 us; the launch traced here: 280 us
  Pallas kernels  111 us (39%)
  waiting for transfers between devices  63.1 us (22%)
  starting transfers between devices  34.5 us (12%)
  local copies, waits for them, and re-layouts  34.4 us (12%)
  other arithmetic  24 us (8%)
  matrix products  10.6 us (4%)
  between operations  2.92 us (1%)
    ppermute x38, waiting for transfers between devices, swap(): return lax.ppermute(value, AXES, pairs)  63.1 us
    ppermute x38, starting transfers between devices, swap(): return lax.ppermute(value, AXES, pairs)  34.5 us
    pallas_call x2, Pallas kernels, run_attend_backward(): pl.pallas_call(attend_backward, grid_spec=pltpu.PrefetchScalarGridSpec(nu...  29.5 us
    pallas_call x1, Pallas kernels, run_feed_forward(): pl.pallas_call(functools.partial(feed_forward, seq, 1024), grid_spec=pltp...  25.4 us
    unnamed x128, local copies, waits for them, and re-layouts  22.6 us
    pallas_call x2, Pallas kernels, run_attend_forward(): pl.pallas_call(attend_forward, grid=(rows // seq, pairs), in_specs=[part(...  18.9 us
    pallas_call x1, Pallas kernels, run_first_gradient(): pl.pallas_call(first_gradient, grid=(rows // block,), in_specs=[token(ff)...  15.7 us
    pallas_call x2, Pallas kernels, run_weight_pieces(): pl.pallas_call(functools.partial(weight_pieces, groups, group_rows), grid...  14.3 us
  transfers between devices with their start and end apart: 38, of which 15 were waited for; matrix products, arithmetic and copies ran while one was open for 11% of the time, Pallas kernels for 25%

profile of v2, /device:TPU:0, one launch (start us, length us, event | category | flops | bytes accessed | tf_op | source)
XLA Modules:
  0.0 280.3 jit_solution(15424502764717328531)
XLA Ops:
  1.4 2.9 %collective-permute-start.1 = (bf16[1152]{0:T(1024)(128)(2,1)S(1)}, bf16[1152]{0:T(1024)(128)(2,1)S(1)}, u32[]{:S(2)}, u32[]{:S(2)}) collective-permute-start(bf16[1152]{0:T(1024)(128)(2,1)S(1)} %get-tuple-element.261), channel_id=1, source_target_pairs={{0,1},{1,0},{2,3},{3,2},{4,5},{5,4},{6,7},{7,6},{8,9},{9,8},{10,11... | collective-permute-start | bytes 6920 | tf_op jit(solution)/shard_map/ppermute | solution.py:497
  9.7 3.9 %fusion.q_ref.k_ref.v_ref = bf16[1024,1152]{1,0:T(8,128)(2,1)S(1)} fusion(bf16[1024,768]{1,0:T(8,128)(2,1)S(1)} %copy-done.17, bf16[768,1152]{1,0:T(8,128)(2,1)} %copy-done.47, f32[1152]{0:T(1024)S(1)} %get-tuple-element.260), kind=kOutput, calls=%fused_computation.2 | convolution fusion | flops 1814298624 | bytes 5706240 | tf_op jit(solution)/shard_map/dot_general | solution.py:26
  13.7 9.7 %attend_forward.2 = (bf16[1024,384]{1,0:T(8,128)(2,1)S(1)}, f32[2,3,2,512]{3,2,1,0:T(2,128)S(1)}) custom-call(bf16[1024,1152]{1,0:T(8,128)(2,1)S(1)} %fusion.q_ref.k_ref.v_ref, bf16[1024,1152]{1,0:T(8,128)(2,1)S(1)} %fusion.q_ref.k_ref.v_ref, bf16[1024,1152]{1,0:T(8,128)(2,1)S(1)} %fusion.q_ref.k_ref.v_ref, s32[2,512,1]{2,1,0:T(8,128)S(1)} %copy.40.lab_ref), custom_call_target="tpu_custom_call" | custom-call | flops 3221225472 | bytes 4194304 | tf_op jit(solution)/shard_map/attend_forward/pallas_call | solution.py:63
  24.3 6.1 %collective-permute-done = bf16[384,1152]{1,0:T(8,128)(2,1)} collective-permute-done((bf16[384,1152]{1,0:T(8,128)(2,1)}, bf16[384,1152]{1,0:T(8,128)(2,1)}, u32[]{:S(2)}, u32[]{:S(2)}) %collective-permute-start) | collective-permute-done | bytes 884768 | tf_op jit(solution)/shard_map/ppermute | solution.py:497
  31.5 1.7 collective-permute-done.2
  33.2 1.6 broadcast_select_fusion.3
  34.8 2.2 fusion.1.q_ref.k_ref.v_ref
  37.1 9.2 %attend_forward.3 = (bf16[1024,384]{1,0:T(8,128)(2,1)S(1)}, f32[2,3,2,512]{3,2,1,0:T(2,128)S(1)}) custom-call(bf16[1024,1152]{1,0:T(8,128)(2,1)S(1)} %fusion.1.q_ref.k_ref.v_ref, bf16[1024,1152]{1,0:T(8,128)(2,1)S(1)} %fusion.1.q_ref.k_ref.v_ref, bf16[1024,1152]{1,0:T(8,128)(2,1)S(1)} %fusion.1.q_ref.k_ref.v_ref, s32[2,512,1]{2,1,0:T(8,128)S(1)} %copy.40.lab_ref), custom_call_target="tpu_custom_call" | custom-call | flops 3221225472 | bytes 4194304 | tf_op jit(solution)/shard_map/attend_forward/pallas_call | solution.py:63
  46.3 25.4 %feed_forward.1 = (bf16[1024,768]{1,0:T(8,128)(2,1)}, bf16[1024,768]{1,0:T(8,128)(2,1)S(1)}, f32[1024,768]{1,0:T(8,128)}, f32[1024,128]{1,0:T(8,128)S(1)}, bf16[...) custom-call(s32[1]{0:T(128)S(6)} %copy.70.count, ...), custom_call_target="tpu_custom_call" | custom-call | flops 21743271936 | bytes 31457280 | tf_op jit(solution)/shard_map/feed_forward/pallas_call | solution.py:299
  71.8 7.2 %weight_pieces.2 = (bf16[8,192,768]{2,1,0:T(8,128)(2,1)S(1)}, bf16[8,192,768]{2,1,0:T(8,128)(2,1)}) custom-call(s32[1]{0:T(128)} %bitcast.6.core_ref, bf16[1024,3072]{1,0:T(8,128)(2,1)S(1)} %get-tuple-element.118.left, bf16[1024,768]{1,0:T(8,128)(2,1)S(1)} %get-tuple-element.129.right.mid_low), custom_call_target="tpu_custom_call" | custom-call | flops 9663676416 | bytes 12582912 | tf_op jit(solution)/shard_map/weight_pieces/pallas_call | solution.py:352
  79.2 2.8 copy-done.3
  82.0 2.3 copy-done.5
  85.8 3.7 %inner_gradient.2 = (bf16[1024,3072]{1,0:T(8,128)(2,1)S(1)}, f32[1,1536]{1,0:T(1,128)S(1)}) custom-call(bf16[1024,768]{1,0:T(8,128)(2,1)S(1)} %copy-done.8, bf16[3072,768]{1,0:T(8,128)(2,1)S(1)} %copy-done.5, bf16[1024,3072]{1,0:T(8,128)(2,1)S(1)} %copy-done.3), custom_call_target="tpu_custom_call" | custom-call | flops 4831838208 | bytes 16777216 | tf_op jit(solution)/shard_map/inner_gradient/pallas_call | solution.py:382
  89.4 2.5 add.208
  92.6 1.6 collective-permute-start.5
  95.6 3.5 %inner_gradient.3 = (bf16[1024,3072]{1,0:T(8,128)(2,1)S(1)}, f32[1,1536]{1,0:T(1,128)S(1)}) custom-call(bf16[1024,768]{1,0:T(8,128)(2,1)S(1)} %copy-done.9, bf16[3072,768]{1,0:T(8,128)(2,1)S(1)} %bitcast.138, bf16[1024,3072]{1,0:T(8,128)(2,1)S(1)} %copy-done.3, bf16[1024,3072]{1,0:T(8,128)(2,1)S(1)} %get-tuple-element.130.refs_0_), custom_call_target="tpu_custom_call", output_to_operand_aliasing={{0}: (3, {})} | custom-call | flops 4831838208 | bytes 16777216 | tf_op jit(solution)/shard_map/inner_gradient/pallas_call | solution.py:382
  99.1 7.1 %weight_pieces.3 = (bf16[8,192,768]{2,1,0:T(8,128)(2,1)S(1)}, bf16[8,192,768]{2,1,0:T(8,128)(2,1)}) custom-call(s32[1]{0:T(128)} %bitcast.6.core_ref, bf16[1024,3072]{1,0:T(8,128)(2,1)S(1)} %get-tuple-element.140.left.grad_inner, bf16[1024,768]{1,0:T(8,128)(2,1)S(1)} %copy-done.38), custom_call_target="tpu_custom_call" | custom-call | flops 9663676416 | bytes 12582912 | tf_op jit(solution)/shard_map/weight_pieces/pallas_call | solution.py:352
  108.3 1.7 collective-permute-done.4
  113.8 2.3 copy-done.16
  116.1 1.9 copy-done.35
  118.0 1.9 copy-done.36
  119.9 15.7 %first_gradient.1 = (f32[1024,768]{1,0:T(8,128)S(1)}, bf16[1024,384]{1,0:T(8,128)(2,1)S(1)}, bf16[1024,384]{1,0:T(8,128)(2,1)S(1)}, bf16[768,768]{1,0:T(8,128)(2,1)S(1)}, f32[8,768]{1,0:T(8,128)S(1)}) custom-call(bf16[1024,3072]{1,0:T(8,128)(2,1)} %copy-done.4, f32[1024,768]{1,0:T(8,128)S(1)} %copy-done.36, bf16[768,3072]{1,0:T(8,128)(2,1)S(1)} %copy-done.16, ...), custom_call_target="tpu_custom_call" | custom-call | flops 14495514624 | bytes 25165824 | tf_op jit(solution)/shard_map/first_gradient/pallas_call | solution.py:454
  138.5 2.9 %add.215 = bf16[8,192,768]{2,1,0:T(8,128)(2,1)S(1)} add(bf16[8,192,768]{2,1,0:T(8,128)(2,1)} %copy-done.6, bf16[8,192,768]{2,1,0:T(8,128)(2,1)} %collective-permute-done.8) | non-fusion elementwise | flops 1179648 | bytes 7077888 | tf_op jit(solution)/shard_map/add | solution.py:512
  145.2 1.7 collective-permute-start.10
  149.9 1.8 bitcast_add_fusion.9
  151.7 1.6 collective-permute-start.11
  153.4 14.7 %attend_backward.2 = (bf16[1024,1152]{1,0:T(8,128)(2,1)S(1)}, bf16[384,1280]{1,0:T(8,128)(2,1)S(1)}, bf16[384,1280]{1,0:T(8,128)(2,1)S(1)}) custom-call(s32[1]{0:T(128)} %bitcast.6.core_ref, bf16[1024,1152]{1,0:T(8,128)(2,1)S(1)} %copy-done.23, bf16[1024,1152]{1,0:T(8,128)(2,1)S(1)} %copy-done.23, bf16[1024,1152]{1,0:T(8,128)(2,1)S(1)} %copy-done.23, ...), custom_call_target="tpu_custom_call" | custom-call | flops 4831838208 | bytes 8388608 | tf_op jit(solution)/shard_map/attend_backward/pallas_call | solution.py:170
  168.3 2.6 collective-permute-start.19
  174.5 2.2 fusion.2
  179.3 14.7 %attend_backward.3 = (bf16[1024,1152]{1,0:T(8,128)(2,1)S(1)}, bf16[384,1280]{1,0:T(8,128)(2,1)S(1)}, bf16[384,1280]{1,0:T(8,128)(2,1)S(1)}) custom-call(s32[1]{0:T(128)} %bitcast.6.core_ref, bf16[1024,1152]{1,0:T(8,128)(2,1)S(1)} %copy-done.21, bf16[1024,1152]{1,0:T(8,128)(2,1)S(1)} %copy-done.21, bf16[1024,1152]{1,0:T(8,128)(2,1)S(1)} %copy-done.21, ...), custom_call_target="tpu_custom_call" | custom-call | flops 4831838208 | bytes 8388608 | tf_op jit(solution)/shard_map/attend_backward/pallas_call | solution.py:170
  196.2 1.7 collective-permute-start.22
  197.9 2.2 fusion.25
  200.1 2.1 add.232
  203.0 4.6 %collective-permute-done.22 = bf16[2,96,768]{2,1,0:T(8,128)(2,1)S(1)} collective-permute-done((bf16[2,96,768]{2,1,0:T(8,128)(2,1)S(1)}, bf16[2,96,768]{2,1,0:T(8,128)(2,1)S(1)}, u32[]{:S(2)}, u32[]{:S(2)}) %collective-permute-start.22) | collective-permute-done | bytes 294944 | tf_op jit(solution)/shard_map/ppermute | solution.py:497
  210.6 2.2 collective-permute-start.25
  212.7 11.5 %collective-permute-done.25 = bf16[96,768]{1,0:T(8,128)(2,1)S(1)} collective-permute-done((bf16[96,768]{1,0:T(8,128)(2,1)S(1)}, bf16[96,768]{1,0:T(8,128)(2,1)S(1)}, u32[]{:S(2)}, u32[]{:S(2)}) %collective-permute-start.25) | collective-permute-done | bytes 147488 | tf_op jit(solution)/shard_map/ppermute | solution.py:497
  226.1 3.5 %collective-permute-done.28 = bf16[48,896]{1,0:T(8,128)(2,1)S(1)} collective-permute-done((bf16[48,896]{1,0:T(8,128)(2,1)S(1)}, bf16[48,896]{1,0:T(8,128)(2,1)S(1)}, u32[]{:S(2)}, u32[]{:S(2)}) %collective-permute-start.28) | collective-permute-done | bytes 86048 | tf_op jit(solution)/shard_map/ppermute | solution.py:497
  229.6 3.2 %collective-permute-done.27 = bf16[96,1280]{1,0:T(8,128)(2,1)S(1)} collective-permute-done((bf16[96,1280]{1,0:T(8,128)(2,1)S(1)}, bf16[96,1280]{1,0:T(8,128)(2,1)S(1)}, u32[]{:S(2)}, u32[]{:S(2)}) %collective-permute-start.27) | collective-permute-done | bytes 245792 | tf_op jit(solution)/shard_map/ppermute | solution.py:497
  234.3 3.6 %collective-permute-done.30 = bf16[48,896]{1,0:T(8,128)(2,1)S(1)} collective-permute-done((bf16[48,896]{1,0:T(8,128)(2,1)S(1)}, bf16[48,896]{1,0:T(8,128)(2,1)S(1)}, u32[]{:S(2)}, u32[]{:S(2)}) %collective-permute-start.30) | collective-permute-done | bytes 86048 | tf_op jit(solution)/shard_map/ppermute | solution.py:497
  237.9 3.0 %collective-permute-done.29 = bf16[48,1280]{1,0:T(8,128)(2,1)S(1)} collective-permute-done((bf16[48,1280]{1,0:T(8,128)(2,1)S(1)}, bf16[48,1280]{1,0:T(8,128)(2,1)S(1)}, u32[]{:S(2)}, u32[]{:S(2)}) %collective-permute-start.29) | collective-permute-done | bytes 122912 | tf_op jit(solution)/shard_map/ppermute | solution.py:497
  241.0 2.0 collective-permute-start.31
  243.0 6.7 %collective-permute-done.31 = bf16[48,1280]{1,0:T(8,128)(2,1)S(1)} collective-permute-done((bf16[48,1280]{1,0:T(8,128)(2,1)S(1)}, bf16[48,1280]{1,0:T(8,128)(2,1)S(1)}, u32[]{:S(2)}, u32[]{:S(2)}) %collective-permute-start.31) | collective-permute-done | bytes 122912 | tf_op jit(solution)/shard_map/ppermute | solution.py:497
  249.9 1.7 collective-permute-start.34
  251.7 6.2 %collective-permute-done.33 = bf16[96,1280]{1,0:T(8,128)(2,1)S(1)} collective-permute-done((bf16[96,1280]{1,0:T(8,128)(2,1)S(1)}, bf16[96,1280]{1,0:T(8,128)(2,1)S(1)}, u32[]{:S(2)}, u32[]{:S(2)}) %collective-permute-start.33) | collective-permute-done | bytes 245792 | tf_op jit(solution)/shard_map/ppermute | solution.py:497
  260.9 1.7 fusion.15
  262.6 1.7 convert_bitcast_fusion
  264.2 9.2 %collective-permute-done.35 = bf16[192,1280]{1,0:T(8,128)(2,1)S(1)} collective-permute-done((bf16[192,1280]{1,0:T(8,128)(2,1)S(1)}, bf16[192,1280]{1,0:T(8,128)(2,1)S(1)}, u32[]{:S(2)}, u32[]{:S(2)}) %collective-permute-start.35) | collective-permute-done | bytes 491552 | tf_op jit(solution)/shard_map/ppermute | solution.py:497
  278.2 1.9 fusion.4
  (277 shorter events, 49.6 us)
Async XLA Ops:
  1.4 22.9 %collective-permute-start.1 = (bf16[1152]{0:T(1024)(128)(2,1)S(1)}, bf16[1152]{0:T(1024)(128)(2,1)S(1)}, u32[]{:S(2)}, u32[]{:S(2)}) collective-permute-start(bf16[1152]{0:T(1024)(128)(2,1)S(1)} %get-tuple-element.261), channel_id=1, source_target_pairs={{0,1},{1,0},{2,3},{3,2},{4,5},{5,4},{6,7},{7,6},{8,9},{9,8},{10,11... | collective-permute-start | bytes 6920 | tf_op jit(solution)/shard_map/ppermute | solution.py:497
  9.0 21.4 %collective-permute-start = (bf16[384,1152]{1,0:T(8,128)(2,1)}, bf16[384,1152]{1,0:T(8,128)(2,1)}, u32[]{:S(2)}, u32[]{:S(2)}) collective-permute-start(bf16[384,1152]{1,0:T(8,128)(2,1)} %dynamic-slice_bitcast_fusion), channel_id=1, source_target_pairs={{0,1},{1,0},{2,3},{3,2},{4,5},{5,4},{6,7},{7,6},{8,9},{9,8},{10,11... | collective-permute-start | bytes 2654216 | tf_op jit(solution)/shard_map/ppermute | solution.py:497
  9.7 27.4 %copy-start.14 = (s32[2,512,1]{2,1,0:T(8,128)}, s32[2,512,1]{2,1,0:T(8,128)S(1)}, u32[]{:S(2)}) copy-start(s32[2,512,1]{2,1,0:T(8,128)S(1)} %copy.40.lab_ref) | copy-start | bytes 12292
  13.6 17.5 %copy-start.55 = (f32[768]{0:T(1024)S(1)}, f32[768]{0:T(1024)}, u32[]{:S(2)}) copy-start(f32[768]{0:T(1024)} %param.29) | copy-start | bytes 9220
  13.6 17.5 %copy-start.56 = (f32[768]{0:T(1024)S(1)}, f32[768]{0:T(1024)}, u32[]{:S(2)}) copy-start(f32[768]{0:T(1024)} %param.28) | copy-start | bytes 9220
  13.6 17.5 %copy-start.57 = (f32[768]{0:T(1024)S(1)}, f32[768]{0:T(1024)}, u32[]{:S(2)}) copy-start(f32[768]{0:T(1024)} %param.30) | copy-start | bytes 9220
  13.6 17.5 %copy-start.58 = (f32[768]{0:T(1024)S(1)}, f32[768]{0:T(1024)}, u32[]{:S(2)}) copy-start(f32[768]{0:T(1024)} %param.34) | copy-start | bytes 9220
  13.6 17.5 %copy-start.59 = (f32[768]{0:T(1024)S(1)}, f32[768]{0:T(1024)}, u32[]{:S(2)}) copy-start(f32[768]{0:T(1024)} %param.35) | copy-start | bytes 9220
  13.7 17.5 %copy-start.60 = (f32[768]{0:T(1024)S(1)}, f32[768]{0:T(1024)}, u32[]{:S(2)}) copy-start(f32[768]{0:T(1024)} %param.36) | copy-start | bytes 9220
  13.7 17.6 %copy-start.49 = (bf16[768,768]{1,0:T(8,128)(2,1)S(1)}, bf16[768,768]{1,0:T(8,128)(2,1)}, u32[]{:S(2)}) copy-start(bf16[768,768]{1,0:T(8,128)(2,1)} %param.27) | copy-start | bytes 3538948
  30.4 2.8 collective-permute-start.2
  31.5 14.9 %copy-start.10 = (bf16[768,768]{1,0:T(8,128)(2,1)}, bf16[768,768]{1,0:T(8,128)(2,1)S(1)}, u32[]{:S(2)}) copy-start(bf16[768,768]{1,0:T(8,128)(2,1)S(1)} %pad_maximum_fusion.2.w_out) | copy-start | bytes 3538948
  46.3 25.5 %copy-start.28 = (bf16[1024,384]{1,0:T(8,128)(2,1)}, bf16[1024,384]{1,0:T(8,128)(2,1)S(1)}, u32[]{:S(2)}) copy-start(bf16[1024,384]{1,0:T(8,128)(2,1)S(1)} %get-tuple-element.116.ctx_b.out_ref) | copy-start | bytes 2359300
  79.0 10.4 %collective-permute-start.3 = (bf16[8,192,768]{2,1,0:T(8,128)(2,1)}, bf16[8,192,768]{2,1,0:T(8,128)(2,1)}, u32[]{:S(2)}, u32[]{:S(2)}) collective-permute-start(bf16[8,192,768]{2,1,0:T(8,128)(2,1)} %get-tuple-element.123), channel_id=1, source_target_pairs={{0,2},{1,3},{2,0},{3,1},{4,6},{5,7},{6,4},{7,5},{8,10},{9,11},{10,... | collective-permute-start | bytes 7077896 | tf_op jit(solution)/shard_map/ppermute | solution.py:497
  92.6 15.7 %collective-permute-start.5 = (bf16[2,2,2,96,384]{4,3,1,0,2:T(8,128)(2,1)S(1)}, bf16[2,2,2,96,384]{4,3,1,0,2:T(8,128)(2,1)S(1)}, u32[]{:S(2)}, u32[]{:S(2)}) collective-permute-start(bf16[2,2,2,96,384]{4,3,1,0,2:T(8,128)(2,1)S(1)} %bitcast.159), channel_id=1, source_target_pairs={{0,4},{1,5},{2,6},{3,7},{4,0},{5,1},{6,2},{7,3},{8,12},{9,13},{10,... | collective-permute-start | bytes 1769480 | tf_op jit(solution)/shard_map/ppermute | solution.py:497
  94.5 15.5 %collective-permute-start.4 = (bf16[2,2,2,96,384]{4,3,1,0,2:T(8,128)(2,1)S(1)}, bf16[2,2,2,96,384]{4,3,1,0,2:T(8,128)(2,1)}, u32[]{:S(2)}, u32[]{:S(2)}) collective-permute-start(bf16[2,2,2,96,384]{4,3,1,0,2:T(8,128)(2,1)S(1)} %bitcast.160), channel_id=1, source_target_pairs={{0,1},{1,0},{2,3},{3,2},{4,5},{5,4},{6,7},{7,6},{8,9},{9,8},{10,11... | collective-permute-start | bytes 1769480 | tf_op jit(solution)/shard_map/ppermute | solution.py:497
  109.9 28.5 %collective-permute-start.8 = (bf16[8,192,768]{2,1,0:T(8,128)(2,1)}, bf16[8,192,768]{2,1,0:T(8,128)(2,1)}, u32[]{:S(2)}, u32[]{:S(2)}) collective-permute-start(bf16[8,192,768]{2,1,0:T(8,128)(2,1)} %get-tuple-element.139), channel_id=1, source_target_pairs={{0,2},{1,3},{2,0},{3,1},{4,6},{5,7},{6,4},{7,5},{8,10},{9,11},{10,... | collective-permute-start | bytes 7077896 | tf_op jit(solution)/shard_map/ppermute | solution.py:497
  110.9 27.6 %collective-permute-start.7 = (bf16[2,2,96,384]{3,2,1,0:T(8,128)(2,1)}, bf16[2,2,96,384]{3,2,1,0:T(8,128)(2,1)}, u32[]{:S(2)}, u32[]{:S(2)}) collective-permute-start(bf16[2,2,96,384]{3,2,1,0:T(8,128)(2,1)} %dynamic-slice_bitcast_fusion.6), channel_id=1, source_target_pairs={{0,1},{1,0},{2,3},{3,2},{4,5},{5,4},{6,7},{7,6},{8,9},{9,8},{10,11... | collective-permute-start | bytes 884744 | tf_op jit(solution)/shard_map/ppermute | solution.py:497
  113.4 25.1 %collective-permute-start.6 = (bf16[2,2,96,384]{3,2,1,0:T(8,128)(2,1)}, bf16[2,2,96,384]{3,2,1,0:T(8,128)(2,1)}, u32[]{:S(2)}, u32[]{:S(2)}) collective-permute-start(bf16[2,2,96,384]{3,2,1,0:T(8,128)(2,1)} %dynamic-slice_bitcast_fusion.7), channel_id=1, source_target_pairs={{0,4},{1,5},{2,6},{3,7},{4,0},{5,1},{6,2},{7,3},{8,12},{9,13},{10,... | collective-permute-start | bytes 884744 | tf_op jit(solution)/shard_map/ppermute | solution.py:497
  145.2 23.0 %collective-permute-start.10 = (bf16[2,2,2,96,384]{4,3,1,0,2:T(8,128)(2,1)S(1)}, bf16[2,2,2,96,384]{4,3,1,0,2:T(8,128)(2,1)S(1)}, u32[]{:S(2)}, u32[]{:S(2)}) collective-permute-start(bf16[2,2,2,96,384]{4,3,1,0,2:T(8,128)(2,1)S(1)} %bitcast.157), channel_id=1, source_target_pairs={{0,4},{1,5},{2,6},{3,7},{4,0},{5,1},{6,2},{7,3},{8,12},{9,13},{10,... | collective-permute-start | bytes 1769480 | tf_op jit(solution)/shard_map/ppermute | solution.py:497
  147.1 21.1 %collective-permute-start.9 = (bf16[2,2,2,96,384]{4,3,1,0,2:T(8,128)(2,1)S(1)}, bf16[2,2,2,96,384]{4,3,1,0,2:T(8,128)(2,1)S(1)}, u32[]{:S(2)}, u32[]{:S(2)}) collective-permute-start(bf16[2,2,2,96,384]{4,3,1,0,2:T(8,128)(2,1)S(1)} %bitcast.158), channel_id=1, source_target_pairs={{0,1},{1,0},{2,3},{3,2},{4,5},{5,4},{6,7},{7,6},{8,9},{9,8},{10,11... | collective-permute-start | bytes 1769480 | tf_op jit(solution)/shard_map/ppermute | solution.py:497
  149.0 19.2 %collective-permute-start.12 = (bf16[192,1792]{1,0:T(8,128)(2,1)S(1)}, bf16[192,1792]{1,0:T(8,128)(2,1)S(1)}, u32[]{:S(2)}, u32[]{:S(2)}) collective-permute-start(bf16[192,1792]{1,0:T(8,128)(2,1)S(1)} %dynamic-slice_bitcast_fusion.1), channel_id=1, source_target_pairs={{0,2},{1,3},{2,0},{3,1},{4,6},{5,7},{6,4},{7,5},{8,10},{9,11},{10,... | collective-permute-start | bytes 2064392 | tf_op jit(solution)/shard_map/ppermute | solution.py:497
  151.7 16.4 %collective-permute-start.11 = (bf16[2,96,768]{2,1,0:T(8,128)(2,1)S(1)}, bf16[2,96,768]{2,1,0:T(8,128)(2,1)S(1)}, u32[]{:S(2)}, u32[]{:S(2)}) collective-permute-start(bf16[2,96,768]{2,1,0:T(8,128)(2,1)S(1)} %fusion.14), channel_id=1, source_target_pairs={{0,8},{1,9},{2,10},{3,11},{4,12},{5,13},{6,14},{7,15},{8,0},{9,1},... | collective-permute-start | bytes 884744 | tf_op jit(solution)/shard_map/ppermute | solution.py:497
  168.3 10.3 %collective-permute-start.19 = (bf16[96,768]{1,0:T(8,128)(2,1)S(1)}, bf16[96,768]{1,0:T(8,128)(2,1)}, u32[]{:S(2)}, u32[]{:S(2)}) collective-permute-start(bf16[96,768]{1,0:T(8,128)(2,1)S(1)} %dynamic-slice_bitcast_fusion.12), channel_id=1, source_target_pairs={{0,16},{1,17},{2,18},{3,19},{4,20},{5,21},{6,22},{7,23},{8,24},{9,... | collective-permute-start | bytes 442376 | tf_op jit(solution)/shard_map/ppermute | solution.py:497
  171.2 22.9 %collective-permute-start.16 = (bf16[2,2,96,384]{3,2,1,0:T(8,128)(2,1)S(1)}, bf16[2,2,96,384]{3,2,1,0:T(8,128)(2,1)S(1)}, u32[]{:S(2)}, u32[]{:S(2)}) collective-permute-start(bf16[2,2,96,384]{3,2,1,0:T(8,128)(2,1)S(1)} %dynamic-slice_bitcast_fusion.5), channel_id=1, source_target_pairs={{0,4},{1,5},{2,6},{3,7},{4,0},{5,1},{6,2},{7,3},{8,12},{9,13},{10,... | collective-permute-start | bytes 884744 | tf_op jit(solution)/shard_map/ppermute | solution.py:497
  171.8 22.3 %collective-permute-start.17 = (bf16[2,2,96,384]{3,2,1,0:T(8,128)(2,1)S(1)}, bf16[2,2,96,384]{3,2,1,0:T(8,128)(2,1)S(1)}, u32[]{:S(2)}, u32[]{:S(2)}) collective-permute-start(bf16[2,2,96,384]{3,2,1,0:T(8,128)(2,1)S(1)} %dynamic-slice_bitcast_fusion.4), channel_id=1, source_target_pairs={{0,1},{1,0},{2,3},{3,2},{4,5},{5,4},{6,7},{7,6},{8,9},{9,8},{10,11... | collective-permute-start | bytes 884744 | tf_op jit(solution)/shard_map/ppermute | solution.py:497
  172.8 4.3 %collective-permute-start.13 = (bf16[384,1280]{1,0:T(8,128)(2,1)S(1)}, bf16[384,1280]{1,0:T(8,128)(2,1)S(1)}, u32[]{:S(2)}, u32[]{:S(2)}) collective-permute-start(bf16[384,1280]{1,0:T(8,128)(2,1)S(1)} %get-tuple-element.164), channel_id=1, source_target_pairs={{0,2},{1,3},{2,0},{3,1},{4,6},{5,7},{6,4},{7,5},{8,10},{9,11},{10,... | collective-permute-start | bytes 2949128 | tf_op jit(solution)/shard_map/ppermute | solution.py:497
  172.9 21.2 %collective-permute-start.18 = (bf16[96,1792]{1,0:T(8,128)(2,1)S(1)}, bf16[96,1792]{1,0:T(8,128)(2,1)S(1)}, u32[]{:S(2)}, u32[]{:S(2)}) collective-permute-start(bf16[96,1792]{1,0:T(8,128)(2,1)S(1)} %dynamic-slice_bitcast_fusion.3), channel_id=1, source_target_pairs={{0,4},{1,5},{2,6},{3,7},{4,0},{5,1},{6,2},{7,3},{8,12},{9,13},{10,... | collective-permute-start | bytes 1032200 | tf_op jit(solution)/shard_map/ppermute | solution.py:497
  177.5 16.6 %collective-permute-start.14 = (bf16[384,640]{1,0:T(8,128)(2,1)S(1)}, bf16[384,640]{1,0:T(8,128)(2,1)S(1)}, u32[]{:S(2)}, u32[]{:S(2)}) collective-permute-start(bf16[384,640]{1,0:T(8,128)(2,1)S(1)} %get-tuple-element.245), channel_id=1, source_target_pairs={{0,1},{1,0},{2,3},{3,2},{4,5},{5,4},{6,7},{7,6},{8,9},{9,8},{10,11... | collective-permute-start | bytes 1474568 | tf_op jit(solution)/shard_map/ppermute | solution.py:497
  178.6 15.5 %collective-permute-start.15 = (bf16[192,640]{1,0:T(8,128)(2,1)S(1)}, bf16[192,640]{1,0:T(8,128)(2,1)S(1)}, u32[]{:S(2)}, u32[]{:S(2)}) collective-permute-start(bf16[192,640]{1,0:T(8,128)(2,1)S(1)} %dynamic-slice_bitcast_fusion.9), channel_id=1, source_target_pairs={{0,4},{1,5},{2,6},{3,7},{4,0},{5,1},{6,2},{7,3},{8,12},{9,13},{10,... | collective-permute-start | bytes 737288 | tf_op jit(solution)/shard_map/ppermute | solution.py:497
  194.3 13.3 %collective-permute-start.21 = (bf16[384,1280]{1,0:T(8,128)(2,1)S(1)}, bf16[384,1280]{1,0:T(8,128)(2,1)S(1)}, u32[]{:S(2)}, u32[]{:S(2)}) collective-permute-start(bf16[384,1280]{1,0:T(8,128)(2,1)S(1)} %get-tuple-element.180), channel_id=1, source_target_pairs={{0,2},{1,3},{2,0},{3,1},{4,6},{5,7},{6,4},{7,5},{8,10},{9,11},{10,... | collective-permute-start | bytes 2949128 | tf_op jit(solution)/shard_map/ppermute | solution.py:497
  194.6 7.6 %collective-permute-start.23 = (bf16[48,1792]{1,0:T(8,128)(2,1)S(1)}, bf16[48,1792]{1,0:T(8,128)(2,1)S(1)}, u32[]{:S(2)}, u32[]{:S(2)}) collective-permute-start(bf16[48,1792]{1,0:T(8,128)(2,1)S(1)} %dynamic-slice_bitcast_fusion.10), channel_id=1, source_target_pairs={{0,8},{1,9},{2,10},{3,11},{4,12},{5,13},{6,14},{7,15},{8,0},{9,1},... | collective-permute-start | bytes 516104 | tf_op jit(solution)/shard_map/ppermute | solution.py:497
  195.1 7.9 %collective-permute-start.20 = (bf16[192,640]{1,0:T(8,128)(2,1)S(1)}, bf16[192,640]{1,0:T(8,128)(2,1)S(1)}, u32[]{:S(2)}, u32[]{:S(2)}) collective-permute-start(bf16[192,640]{1,0:T(8,128)(2,1)S(1)} %bitcast_add_fusion.12), channel_id=1, source_target_pairs={{0,1},{1,0},{2,3},{3,2},{4,5},{5,4},{6,7},{7,6},{8,9},{9,8},{10,11... | collective-permute-start | bytes 737288 | tf_op jit(solution)/shard_map/ppermute | solution.py:497
  196.2 11.3 %collective-permute-start.22 = (bf16[2,96,768]{2,1,0:T(8,128)(2,1)S(1)}, bf16[2,96,768]{2,1,0:T(8,128)(2,1)S(1)}, u32[]{:S(2)}, u32[]{:S(2)}) collective-permute-start(bf16[2,96,768]{2,1,0:T(8,128)(2,1)S(1)} %fusion.9), channel_id=1, source_target_pairs={{0,8},{1,9},{2,10},{3,11},{4,12},{5,13},{6,14},{7,15},{8,0},{9,1},... | collective-permute-start | bytes 884744 | tf_op jit(solution)/shard_map/ppermute | solution.py:497
  207.6 16.6 %collective-permute-start.26 = (bf16[48,1792]{1,0:T(8,128)(2,1)S(1)}, bf16[48,1792]{1,0:T(8,128)(2,1)S(1)}, u32[]{:S(2)}, u32[]{:S(2)}) collective-permute-start(bf16[48,1792]{1,0:T(8,128)(2,1)S(1)} %bitcast_add_fusion.13), channel_id=1, source_target_pairs={{0,16},{1,17},{2,18},{3,19},{4,20},{5,21},{6,22},{7,23},{8,24},{9,... | collective-permute-start | bytes 516104 | tf_op jit(solution)/shard_map/ppermute | solution.py:497
  209.0 15.2 %collective-permute-start.24 = (bf16[192,1280]{1,0:T(8,128)(2,1)S(1)}, bf16[192,1280]{1,0:T(8,128)(2,1)S(1)}, u32[]{:S(2)}, u32[]{:S(2)}) collective-permute-start(bf16[192,1280]{1,0:T(8,128)(2,1)S(1)} %dynamic-slice_bitcast_fusion.2), channel_id=1, source_target_pairs={{0,4},{1,5},{2,6},{3,7},{4,0},{5,1},{6,2},{7,3},{8,12},{9,13},{10,... | collective-permute-start | bytes 1474568 | tf_op jit(solution)/shard_map/ppermute | solution.py:497
  210.6 13.6 %collective-permute-start.25 = (bf16[96,768]{1,0:T(8,128)(2,1)S(1)}, bf16[96,768]{1,0:T(8,128)(2,1)S(1)}, u32[]{:S(2)}, u32[]{:S(2)}) collective-permute-start(bf16[96,768]{1,0:T(8,128)(2,1)S(1)} %dynamic-slice_bitcast_fusion.11), channel_id=1, source_target_pairs={{0,16},{1,17},{2,18},{3,19},{4,20},{5,21},{6,22},{7,23},{8,24},{9,... | collective-permute-start | bytes 442376 | tf_op jit(solution)/shard_map/ppermute | solution.py:497
  224.9 7.9 %collective-permute-start.27 = (bf16[96,1280]{1,0:T(8,128)(2,1)S(1)}, bf16[96,1280]{1,0:T(8,128)(2,1)S(1)}, u32[]{:S(2)}, u32[]{:S(2)}) collective-permute-start(bf16[96,1280]{1,0:T(8,128)(2,1)S(1)} %dynamic-slice_bitcast_fusion.8), channel_id=1, source_target_pairs={{0,8},{1,9},{2,10},{3,11},{4,12},{5,13},{6,14},{7,15},{8,0},{9,1},... | collective-permute-start | bytes 737288 | tf_op jit(solution)/shard_map/ppermute | solution.py:497
  225.0 4.6 %collective-permute-start.28 = (bf16[48,896]{1,0:T(8,128)(2,1)S(1)}, bf16[48,896]{1,0:T(8,128)(2,1)S(1)}, u32[]{:S(2)}, u32[]{:S(2)}) collective-permute-start(bf16[48,896]{1,0:T(8,128)(2,1)S(1)} %slice.167), channel_id=1, source_target_pairs={{0,1},{1,0},{2,3},{3,2},{4,5},{5,4},{6,7},{7,6},{8,9},{9,8},{10,11... | collective-permute-start | bytes 258056 | tf_op jit(solution)/shard_map/ppermute | solution.py:497
  232.9 8.0 %collective-permute-start.29 = (bf16[48,1280]{1,0:T(8,128)(2,1)S(1)}, bf16[48,1280]{1,0:T(8,128)(2,1)S(1)}, u32[]{:S(2)}, u32[]{:S(2)}) collective-permute-start(bf16[48,1280]{1,0:T(8,128)(2,1)S(1)} %dynamic-slice_bitcast_fusion.13), channel_id=1, source_target_pairs={{0,16},{1,17},{2,18},{3,19},{4,20},{5,21},{6,22},{7,23},{8,24},{9,... | collective-permute-start | bytes 368648 | tf_op jit(solution)/shard_map/ppermute | solution.py:497
  233.3 4.6 %collective-permute-start.30 = (bf16[48,896]{1,0:T(8,128)(2,1)S(1)}, bf16[48,896]{1,0:T(8,128)(2,1)S(1)}, u32[]{:S(2)}, u32[]{:S(2)}) collective-permute-start(bf16[48,896]{1,0:T(8,128)(2,1)S(1)} %slice_add_fusion.2), channel_id=1, source_target_pairs={{0,1},{1,0},{2,3},{3,2},{4,5},{5,4},{6,7},{7,6},{8,9},{9,8},{10,11... | collective-permute-start | bytes 258056 | tf_op jit(solution)/shard_map/ppermute | solution.py:497
  240.9 8.9 %collective-permute-start.32 = (bf16[48,1792]{1,0:T(8,128)(2,1)S(1)}, bf16[48,1792]{1,0:T(8,128)(2,1)S(1)}, u32[]{:S(2)}, u32[]{:S(2)}) collective-permute-start(bf16[48,1792]{1,0:T(8,128)(2,1)S(1)} %pad_maximum_fusion.14), channel_id=1, source_target_pairs={{0,8},{1,9},{2,10},{3,11},{4,12},{5,13},{6,14},{7,15},{8,0},{9,1},... | collective-permute-start | bytes 516104 | tf_op jit(solution)/shard_map/ppermute | solution.py:497
  241.0 8.8 %collective-permute-start.31 = (bf16[48,1280]{1,0:T(8,128)(2,1)S(1)}, bf16[48,1280]{1,0:T(8,128)(2,1)S(1)}, u32[]{:S(2)}, u32[]{:S(2)}) collective-permute-start(bf16[48,1280]{1,0:T(8,128)(2,1)S(1)} %bitcast_add_fusion.16), channel_id=1, source_target_pairs={{0,16},{1,17},{2,18},{3,19},{4,20},{5,21},{6,22},{7,23},{8,24},{9,... | collective-permute-start | bytes 368648 | tf_op jit(solution)/shard_map/ppermute | solution.py:497
  249.9 8.7 %collective-permute-start.34 = (bf16[96,1792]{1,0:T(8,128)(2,1)S(1)}, bf16[96,1792]{1,0:T(8,128)(2,1)S(1)}, u32[]{:S(2)}, u32[]{:S(2)}) collective-permute-start(bf16[96,1792]{1,0:T(8,128)(2,1)S(1)} %pad_maximum_fusion.12), channel_id=1, source_target_pairs={{0,4},{1,5},{2,6},{3,7},{4,0},{5,1},{6,2},{7,3},{8,12},{9,13},{10,... | collective-permute-start | bytes 1032200 | tf_op jit(solution)/shard_map/ppermute | solution.py:497
  251.6 6.3 %collective-permute-start.33 = (bf16[96,1280]{1,0:T(8,128)(2,1)S(1)}, bf16[96,1280]{1,0:T(8,128)(2,1)S(1)}, u32[]{:S(2)}, u32[]{:S(2)}) collective-permute-start(bf16[96,1280]{1,0:T(8,128)(2,1)S(1)} %pad_maximum_fusion.13), channel_id=1, source_target_pairs={{0,8},{1,9},{2,10},{3,11},{4,12},{5,13},{6,14},{7,15},{8,0},{9,1},... | collective-permute-start | bytes 737288 | tf_op jit(solution)/shard_map/ppermute | solution.py:497
  259.7 13.7 %collective-permute-start.36 = (bf16[192,1792]{1,0:T(8,128)(2,1)}, bf16[192,1792]{1,0:T(8,128)(2,1)S(1)}, u32[]{:S(2)}, u32[]{:S(2)}) collective-permute-start(bf16[192,1792]{1,0:T(8,128)(2,1)} %pad_maximum_fusion.8), channel_id=1, source_target_pairs={{0,2},{1,3},{2,0},{3,1},{4,6},{5,7},{6,4},{7,5},{8,10},{9,11},{10,... | collective-permute-start | bytes 2064392 | tf_op jit(solution)/shard_map/ppermute | solution.py:497
  259.8 13.7 %collective-permute-start.35 = (bf16[192,1280]{1,0:T(8,128)(2,1)S(1)}, bf16[192,1280]{1,0:T(8,128)(2,1)S(1)}, u32[]{:S(2)}, u32[]{:S(2)}) collective-permute-start(bf16[192,1280]{1,0:T(8,128)(2,1)S(1)} %pad_maximum_fusion.11), channel_id=1, source_target_pairs={{0,4},{1,5},{2,6},{3,7},{4,0},{5,1},{6,2},{7,3},{8,12},{9,13},{10,... | collective-permute-start | bytes 1474568 | tf_op jit(solution)/shard_map/ppermute | solution.py:497
  273.7 3.6 %collective-permute-start.37 = (bf16[384,1280]{1,0:T(8,128)(2,1)S(1)}, bf16[384,1280]{1,0:T(8,128)(2,1)S(1)}, u32[]{:S(2)}, u32[]{:S(2)}) collective-permute-start(bf16[384,1280]{1,0:T(8,128)(2,1)S(1)} %pad_maximum_fusion.6), channel_id=1, source_target_pairs={{0,2},{1,3},{2,0},{3,1},{4,6},{5,7},{6,4},{7,5},{8,10},{9,11},{10,... | collective-permute-start | bytes 2949128 | tf_op jit(solution)/shard_map/ppermute | solution.py:497
  (53 other events, 195.0 us)
